TPU v7x, 512 devices: a whole 4x8x8 slice. The times are simulated.
512 devices in a mesh: context: 32 (over x, z_hi, core), dp: 16 (over z_lo, y).
Axes of the slice: x: 4, y: 8, z: 8 (z_hi: 4, z_lo: 2; z = z_hi * 2 + z_lo), core: 2. Of those that a mesh axis runs over, the one named last changes fastest.
Arguments:
- hyena_in: bfloat16 [32768, 4096], P(('dp', 'context')), parts along dimension 0, may hold values from -6 to 6
- filt: bfloat16 [32768, 128], P(('dp', 'context')), parts along dimension 0, may hold values from -1 to 1
- keys: bfloat16 [32768, 4096], P(('dp', 'context')), parts along dimension 0, may hold values from -81 to 81
- values: bfloat16 [32768, 4096], P(('dp', 'context')), parts along dimension 0, may hold values from -6 to 6
Outputs:
- mixed: bfloat16 [32768, 4096], P(('dp', 'context')), parts along dimension 0
There are 16 independent parts, one for each index of `dp`. A program takes and returns all parts, laid end to end along the dimension named above; each array names one. Nothing has to cross between parts.
All inputs are finite; a program needn't handle non-finite values.
Results may differ from a plain program's by a relative error of at most 0.0089.
Values may be sent and summed in bfloat16 or wider, within the bound.
No kernel may reach another device: no remote copies, remote signals or barrier semaphores. Data moves between devices by JAX's collectives and lax.ppermute only.
A program may use at most 64 MiB of HBM per device.

v0:
```python
import math

import jax
import jax.numpy as jnp
from jax import lax
from jax.sharding import PartitionSpec as P

HEAD_DIM = 128


def passed_along(shard, axis, by):
    peers = lax.axis_size(axis)
    pairs = [(i, i + by) for i in range(peers) if 0 <= i + by < peers]
    return lax.ppermute(shard, axis, pairs)


def tables(rows, cols, period):
    first = jnp.arange(rows, dtype=jnp.int32)[:, None]
    second = jnp.arange(cols, dtype=jnp.int32)[None, :]
    phase = first * second % period
    angle = phase.astype(jnp.float32) * (2.0 * math.pi / period)
    return (jnp.cos(angle), jnp.sin(angle))


def matmul(left, right):
    return jnp.dot(left, right, precision=lax.Precision.HIGHEST, preferred_element_type=jnp.float32)


def move_blocks(keys, values):
    current = (keys, values)
    earlier = []
    for step in range(2):
        current = passed_along((current[0], current[1]), "context", 1)
        earlier.append(current)
    return (earlier[0], earlier[1])


def local(hyena_in, filt, keys, values):
    parts = lax.axis_size("context")
    device = lax.axis_index("context")
    tok, width = hyena_in.shape
    groups = filt.shape[1]
    half = width // 2
    per = tok // parts
    span = 2 * tok
    share = span // parts
    total = span * parts

    def cyclic_form(array):
        return array.reshape(1, per, parts, array.shape[1])

    moved_in, moved_filt = (
        lax.all_to_all(cyclic_form(hyena_in), "context", split_axis=2, concat_axis=0, tiled=True),
        lax.all_to_all(cyclic_form(filt), "context", split_axis=2, concat_axis=0, tiled=True),
    )
    joined = jnp.concatenate(
        [
            moved_in.reshape(tok, width).astype(jnp.float32),
            moved_filt.reshape(tok, groups).astype(jnp.float32),
        ],
        axis=1,
    )
    cos_one, sin_one = tables(span, tok, span)
    real_part = matmul(cos_one, joined)
    imag_part = -matmul(sin_one, joined)
    spec_re = jnp.concatenate(
        [real_part[:, :half] - imag_part[:, half:width], real_part[:, width:]], axis=1
    )
    spec_im = jnp.concatenate(
        [imag_part[:, :half] + real_part[:, half:width], imag_part[:, width:]], axis=1
    )
    freq = jnp.arange(span, dtype=jnp.int32)
    twist = (device * freq % total).astype(jnp.float32) * (2.0 * math.pi / total)
    twist_cos = jnp.cos(twist)[:, None]
    twist_sin = jnp.sin(twist)[:, None]
    turned_re = spec_re * twist_cos + spec_im * twist_sin
    turned_im = spec_im * twist_cos - spec_re * twist_sin
    width_all = half + groups
    got_re, got_im = (
        lax.all_to_all(
            turned_re.reshape(span, 1, width_all),
            "context",
            split_axis=0,
            concat_axis=1,
            tiled=True,
        ),
        lax.all_to_all(
            turned_im.reshape(span, 1, width_all),
            "context",
            split_axis=0,
            concat_axis=1,
            tiled=True,
        ),
    )
    cos_two, sin_two = tables(parts, parts, parts)
    hp = lax.Precision.HIGHEST
    full_re = jnp.einsum("kq,rqc->rkc", cos_two, got_re, precision=hp) + jnp.einsum(
        "kq,rqc->rkc", sin_two, got_im, precision=hp
    )
    full_im = jnp.einsum("kq,rqc->rkc", cos_two, got_im, precision=hp) - jnp.einsum(
        "kq,rqc->rkc", sin_two, got_re, precision=hp
    )
    repeat = half // groups
    data_re = full_re[:, :, :half].reshape(share, parts, repeat, groups)
    data_im = full_im[:, :, :half].reshape(share, parts, repeat, groups)
    filt_re = full_re[:, :, half:][:, :, None, :]
    filt_im = full_im[:, :, half:][:, :, None, :]
    prod_re = (data_re * filt_re - data_im * filt_im).reshape(share, parts, half)
    prod_im = (data_re * filt_im + data_im * filt_re).reshape(share, parts, half)
    back_re = jnp.einsum("qk,rkc->rqc", cos_two, prod_re, precision=hp) - jnp.einsum(
        "qk,rkc->rqc", sin_two, prod_im, precision=hp
    )
    back_im = jnp.einsum("qk,rkc->rqc", cos_two, prod_im, precision=hp) + jnp.einsum(
        "qk,rkc->rqc", sin_two, prod_re, precision=hp
    )
    ret_re, ret_im = (
        lax.all_to_all(back_re, "context", split_axis=1, concat_axis=0, tiled=True),
        lax.all_to_all(back_im, "context", split_axis=1, concat_axis=0, tiled=True),
    )
    ret_re = ret_re.reshape(span, half)
    ret_im = ret_im.reshape(span, half)
    unturned_re = ret_re * twist_cos - ret_im * twist_sin
    unturned_im = ret_re * twist_sin + ret_im * twist_cos
    cos_three, sin_three = tables(tok, span, span)
    norm = 1.0 / total
    conv_lo = (matmul(cos_three, unturned_re) - matmul(sin_three, unturned_im)) * norm
    conv_hi = (matmul(sin_three, unturned_re) + matmul(cos_three, unturned_im)) * norm
    conv = jnp.concatenate([conv_lo, conv_hi], axis=1).astype(jnp.bfloat16)
    queries = lax.all_to_all(
        conv.reshape(parts, per, 1, width), "context", split_axis=0, concat_axis=2, tiled=True
    ).reshape(tok, width)
    near_pair, far_pair = move_blocks(keys, values)
    heads = width // HEAD_DIM
    key_all = jnp.concatenate([far_pair[0], near_pair[0], keys], axis=0).reshape(
        3 * tok, heads, HEAD_DIM
    )
    val_all = jnp.concatenate([far_pair[1], near_pair[1], values], axis=0).reshape(
        3 * tok, heads, HEAD_DIM
    )
    query_heads = queries.reshape(tok, heads, HEAD_DIM)
    scores = jnp.einsum(
        "qhd,khd->hqk", query_heads, key_all, preferred_element_type=jnp.float32
    ) * (1.0 / math.sqrt(HEAD_DIM))
    rows = jnp.arange(tok, dtype=jnp.int32)[:, None]
    cols = jnp.arange(3 * tok, dtype=jnp.int32)[None, :]
    allowed = (cols >= (2 - device) * tok) & (cols <= 2 * tok + rows)
    scores = jnp.where(allowed[None], scores, -1e30)
    top = jnp.max(scores, axis=-1, keepdims=True)
    expo = jnp.where(allowed[None], jnp.exp(scores - top), 0.0)
    probs = (expo / jnp.sum(expo, axis=-1, keepdims=True)).astype(jnp.bfloat16)
    out = jnp.einsum("hqk,khd->qhd", probs, val_all, preferred_element_type=jnp.float32)
    return out.astype(jnp.bfloat16).reshape(tok, width)


def solution(mesh):
    return jax.shard_map(
        local,
        mesh=mesh,
        in_specs=(
            P(("dp", "context"), None),
            P(("dp", "context"), None),
            P(("dp", "context"), None),
            P(("dp", "context"), None),
        ),
        out_specs=P(("dp", "context"), None),
        check_vma=False,
    )
```

profile of v0, /device:TPU:126, one launch (start us, length us, event | category | flops | bytes accessed | tf_op | source)
XLA Modules:
  0.0 268.5 jit_solution(16415917102353494192)
XLA Ops:
  0.0 2.4 copy.30
  2.4 12.5 %all-to-all-start = ((bf16[1,2,32,4096]{3,1,0,2:T(2,128)(2,1)}), bf16[1,2,32,4096]{3,1,0,2:T(2,128)(2,1)S(1)}, u32[]{:S(2)}, u32[]{:S(2)}) async-start(bf16[1,2,32,4096]{3,1,0,2:T(2,128)(2,1)} %copy.30), calls=%async_computation | async-start | bytes 1048576 | tf_op jit(solution)/shard_map/all_to_all | solution.py:53
  15.6 16.1 %all-to-all-done = bf16[1,2,32,4096]{3,1,0,2:T(2,128)(2,1)S(1)} async-done(((bf16[1,2,32,4096]{3,1,0,2:T(2,128)(2,1)}), bf16[1,2,32,4096]{3,1,0,2:T(2,128)(2,1)S(1)}, u32[]{:S(2)}, u32[]{:S(2)}) %all-to-all-start) | async-done | bytes 524320 | tf_op jit(solution)/shard_map/all_to_all | solution.py:53
  31.7 6.3 %all-to-all-start.1 = ((bf16[1,2,32,128]{3,1,0,2:T(2,128)(2,1)}), bf16[1,2,32,128]{3,1,0,2:T(2,128)(2,1)S(1)}, u32[]{:S(2)}, u32[]{:S(2)}) async-start(bf16[1,2,32,128]{3,1,0,2:T(2,128)(2,1)} %copy.31), calls=%async_computation.1 | async-start | bytes 32768 | tf_op jit(solution)/shard_map/all_to_all | solution.py:54
  38.2 7.6 %all-to-all-done.1 = bf16[1,2,32,128]{3,1,0,2:T(2,128)(2,1)S(1)} async-done(((bf16[1,2,32,128]{3,1,0,2:T(2,128)(2,1)}), bf16[1,2,32,128]{3,1,0,2:T(2,128)(2,1)S(1)}, u32[]{:S(2)}, u32[]{:S(2)}) %all-to-all-start.1) | async-done | bytes 16416 | tf_op jit(solution)/shard_map/all_to_all | solution.py:54
  45.8 1.2 convolution_negate_fusion
  47.1 1.2 fusion.38
  49.0 2.1 copy.32
  51.1 5.8 %all-to-all-start.2 = ((f32[128,1,2176]{2,1,0:T(1,128)}), f32[128,1,2176]{2,1,0:T(1,128)S(1)}, u32[]{:S(2)}, u32[]{:S(2)}) async-start(f32[128,1,2176]{2,1,0:T(1,128)} %copy.32), calls=%async_computation.2 | async-start | bytes 2228224 | tf_op jit(solution)/shard_map/all_to_all | solution.py:80
  56.9 2.2 copy.34
  59.1 26.7 %all-to-all-done.2 = f32[128,1,2176]{2,1,0:T(1,128)S(1)} async-done(((f32[128,1,2176]{2,1,0:T(1,128)}), f32[128,1,2176]{2,1,0:T(1,128)S(1)}, u32[]{:S(2)}, u32[]{:S(2)}) %all-to-all-start.2) | async-done | bytes 1114144 | tf_op jit(solution)/shard_map/all_to_all | solution.py:80
  85.8 6.0 %all-to-all-start.3 = ((f32[128,1,2176]{2,1,0:T(1,128)}), f32[128,1,2176]{2,1,0:T(1,128)S(1)}, u32[]{:S(2)}, u32[]{:S(2)}) async-start(f32[128,1,2176]{2,1,0:T(1,128)} %copy.34), calls=%async_computation.3 | async-start | bytes 2228224 | tf_op jit(solution)/shard_map/all_to_all | solution.py:87
  91.8 2.1 fusion.23
  94.0 26.7 %all-to-all-done.3 = f32[128,1,2176]{2,1,0:T(1,128)S(1)} async-done(((f32[128,1,2176]{2,1,0:T(1,128)}), f32[128,1,2176]{2,1,0:T(1,128)S(1)}, u32[]{:S(2)}, u32[]{:S(2)}) %all-to-all-start.3) | async-done | bytes 1114144 | tf_op jit(solution)/shard_map/all_to_all | solution.py:87
  120.6 1.1 fusion.25
  121.9 1.2 fusion.1
  123.1 1.0 copy-done.1
  124.1 1.1 mul.333
  125.3 1.2 fusion.2
  126.4 1.0 copy-done.3
  127.5 1.1 mul.336
  129.1 2.1 multiply_subtract_fusion.2
  131.3 1.1 fusion.65
  132.4 1.1 fusion.4
  133.5 1.6 copy.36
  135.2 6.0 %all-to-all-start.4 = ((f32[4,32,2048]{2,0,1:T(4,128)}), f32[4,32,2048]{2,0,1:T(4,128)S(1)}, u32[]{:S(2)}, u32[]{:S(2)}) async-start(f32[4,32,2048]{2,0,1:T(4,128)} %copy.36), calls=%async_computation.4 | async-start | bytes 2097152 | tf_op jit(solution)/shard_map/all_to_all | solution.py:117
  141.1 1.1 fusion.63
  142.3 1.1 fusion.3
  143.4 1.7 copy.37
  145.1 23.5 %all-to-all-done.4 = f32[4,32,2048]{2,0,1:T(4,128)S(1)} async-done(((f32[4,32,2048]{2,0,1:T(4,128)}), f32[4,32,2048]{2,0,1:T(4,128)S(1)}, u32[]{:S(2)}, u32[]{:S(2)}) %all-to-all-start.4) | async-done | bytes 1048608 | tf_op jit(solution)/shard_map/all_to_all | solution.py:117
  168.6 6.8 %all-to-all-start.5 = ((f32[4,32,2048]{2,0,1:T(4,128)}), f32[4,32,2048]{2,0,1:T(4,128)}, u32[]{:S(2)}, u32[]{:S(2)}) async-start(f32[4,32,2048]{2,0,1:T(4,128)} %copy.37), calls=%async_computation.5 | async-start | bytes 2097152 | tf_op jit(solution)/shard_map/all_to_all | solution.py:118
  175.4 2.1 collective-permute-start.2
  177.8 27.6 %all-to-all-done.5 = f32[4,32,2048]{2,0,1:T(4,128)} async-done(((f32[4,32,2048]{2,0,1:T(4,128)}), f32[4,32,2048]{2,0,1:T(4,128)}, u32[]{:S(2)}, u32[]{:S(2)}) %all-to-all-start.5) | async-done | bytes 1048608 | tf_op jit(solution)/shard_map/all_to_all | solution.py:118
  205.4 1.6 reshape.345
  207.0 1.0 fusion.74
  207.9 1.0 fusion.76
  208.9 1.0 fusion.8
  210.1 1.0 fusion.7
  211.3 1.4 pad_maximum_fusion.3
  212.7 7.6 %all-to-all-start.6 = ((bf16[32,2,1,4096]{3,1,2,0:T(2,128)(2,1)}), bf16[32,2,1,4096]{3,1,2,0:T(2,128)(2,1)S(1)}, u32[]{:S(2)}, u32[]{:S(2)}) async-start(bf16[32,2,1,4096]{3,1,2,0:T(2,128)(2,1)} %pad_maximum_fusion.3), calls=%async_computation.6 | async-start | bytes 1048576 | tf_op jit(solution)/shard_map/all_to_all | solution.py:129
  220.4 2.1 collective-permute-start
  222.4 4.2 %collective-permute-start.3 = (bf16[64,4096]{1,0:T(8,128)(2,1)}, bf16[64,4096]{1,0:T(8,128)(2,1)S(1)}, u32[]{:S(2)}, u32[]{:S(2)}) collective-permute-start(bf16[64,4096]{1,0:T(8,128)(2,1)} %collective-permute-done.2), channel_id=1, source_target_pairs={{0,16},{16,32},{32,48},{48,64},{64,80},{80,96},{96,112},{112,128},... | collective-permute-start | bytes 1572872 | tf_op jit(solution)/shard_map/ppermute | solution.py:14
  226.7 24.1 %collective-permute-done = bf16[64,4096]{1,0:T(8,128)(2,1)S(1)} collective-permute-done((bf16[64,4096]{1,0:T(8,128)(2,1)S(1)}, bf16[64,4096]{1,0:T(8,128)(2,1)S(1)}, u32[]{:S(2)}, u32[]{:S(2)}) %collective-permute-start) | collective-permute-done | bytes 524320 | tf_op jit(solution)/shard_map/ppermute | solution.py:14
  250.8 1.9 collective-permute-start.1
  253.2 4.0 %collective-permute-done.3 = bf16[64,4096]{1,0:T(8,128)(2,1)S(1)} collective-permute-done((bf16[64,4096]{1,0:T(8,128)(2,1)}, bf16[64,4096]{1,0:T(8,128)(2,1)S(1)}, u32[]{:S(2)}, u32[]{:S(2)}) %collective-permute-start.3) | collective-permute-done | bytes 524320 | tf_op jit(solution)/shard_map/ppermute | solution.py:14
  257.2 3.9 %fusion.167 = (f32[32,64]{1,0:T(8,128)S(1)}, f32[32,64,192]{2,1,0:T(8,128)}) fusion(pred[64,192]{1,0:T(8,128)(4,1)S(1)} %fusion.47, bf16[64,32,128]{2,1,0:T(8,128)(2,1)S(1)} %bitcast.134, bf16[64,4096]{1,0:T(8,128)(2,1)} %param.6, bf16[64,4096]{1,0:T(8,128)(2,1)} %collective-permute-done.2, bf16[64,4096]{1,0:T(8,128)(2,1)S(1)} %collective-permute-done.3), kind=kOutput, calls=%fused_computation.179 | convolution fusion | flops 107348160 | bytes 3690496 | tf_op jit(solution)/shard_map/sub | solution.py:149
  261.1 4.2 %collective-permute-done.1 = bf16[64,4096]{1,0:T(8,128)(2,1)S(1)} collective-permute-done((bf16[64,4096]{1,0:T(8,128)(2,1)S(1)}, bf16[64,4096]{1,0:T(8,128)(2,1)S(1)}, u32[]{:S(2)}, u32[]{:S(2)}) %collective-permute-start.1) | collective-permute-done | bytes 524320 | tf_op jit(solution)/shard_map/ppermute | solution.py:14
  265.3 2.3 fusion.19
  (31 shorter events, 4.3 us)
Async XLA Ops:
  0.0 14.9 %copy-start.4 = (bf16[64,128]{1,0:T(8,128)(2,1)S(1)}, bf16[64,128]{1,0:T(8,128)(2,1)}, u32[]{:S(2)}) copy-start(bf16[64,128]{1,0:T(8,128)(2,1)} %param.5) | copy-start | bytes 49156
  2.4 29.3 %all-to-all-start = ((bf16[1,2,32,4096]{3,1,0,2:T(2,128)(2,1)}), bf16[1,2,32,4096]{3,1,0,2:T(2,128)(2,1)S(1)}, u32[]{:S(2)}, u32[]{:S(2)}) async-start(bf16[1,2,32,4096]{3,1,0,2:T(2,128)(2,1)} %copy.30), calls=%async_computation | async-start | bytes 1048576 | tf_op jit(solution)/shard_map/all_to_all | solution.py:53
  31.7 14.2 %all-to-all-start.1 = ((bf16[1,2,32,128]{3,1,0,2:T(2,128)(2,1)}), bf16[1,2,32,128]{3,1,0,2:T(2,128)(2,1)S(1)}, u32[]{:S(2)}, u32[]{:S(2)}) async-start(bf16[1,2,32,128]{3,1,0,2:T(2,128)(2,1)} %copy.31), calls=%async_computation.1 | async-start | bytes 32768 | tf_op jit(solution)/shard_map/all_to_all | solution.py:54
  51.1 34.7 %all-to-all-start.2 = ((f32[128,1,2176]{2,1,0:T(1,128)}), f32[128,1,2176]{2,1,0:T(1,128)S(1)}, u32[]{:S(2)}, u32[]{:S(2)}) async-start(f32[128,1,2176]{2,1,0:T(1,128)} %copy.32), calls=%async_computation.2 | async-start | bytes 2228224 | tf_op jit(solution)/shard_map/all_to_all | solution.py:80
  85.8 34.8 %all-to-all-start.3 = ((f32[128,1,2176]{2,1,0:T(1,128)}), f32[128,1,2176]{2,1,0:T(1,128)S(1)}, u32[]{:S(2)}, u32[]{:S(2)}) async-start(f32[128,1,2176]{2,1,0:T(1,128)} %copy.34), calls=%async_computation.3 | async-start | bytes 2228224 | tf_op jit(solution)/shard_map/all_to_all | solution.py:87
  120.6 1.2 copy-start
  123.0 1.0 copy-start.1
  126.4 1.0 copy-start.3
  127.5 1.6 copy-start.2
  135.2 33.4 %all-to-all-start.4 = ((f32[4,32,2048]{2,0,1:T(4,128)}), f32[4,32,2048]{2,0,1:T(4,128)S(1)}, u32[]{:S(2)}, u32[]{:S(2)}) async-start(f32[4,32,2048]{2,0,1:T(4,128)} %copy.36), calls=%async_computation.4 | async-start | bytes 2097152 | tf_op jit(solution)/shard_map/all_to_all | solution.py:117
  168.6 36.8 %all-to-all-start.5 = ((f32[4,32,2048]{2,0,1:T(4,128)}), f32[4,32,2048]{2,0,1:T(4,128)}, u32[]{:S(2)}, u32[]{:S(2)}) async-start(f32[4,32,2048]{2,0,1:T(4,128)} %copy.37), calls=%async_computation.5 | async-start | bytes 2097152 | tf_op jit(solution)/shard_map/all_to_all | solution.py:118
  175.4 47.1 %collective-permute-start.2 = (bf16[64,4096]{1,0:T(8,128)(2,1)}, bf16[64,4096]{1,0:T(8,128)(2,1)}, u32[]{:S(2)}, u32[]{:S(2)}) collective-permute-start(bf16[64,4096]{1,0:T(8,128)(2,1)} %param.6), channel_id=1, source_target_pairs={{0,16},{16,32},{32,48},{48,64},{64,80},{80,96},{96,112},{112,128},... | collective-permute-start | bytes 1572872 | tf_op jit(solution)/shard_map/ppermute | solution.py:14
  211.3 9.1 %copy-start.5 = (bf16[64,4096]{1,0:T(8,128)(2,1)S(1)}, bf16[64,4096]{1,0:T(8,128)(2,1)}, u32[]{:S(2)}) copy-start(bf16[64,4096]{1,0:T(8,128)(2,1)} %param.7) | copy-start | bytes 1572868
  212.7 40.1 %all-to-all-start.6 = ((bf16[32,2,1,4096]{3,1,2,0:T(2,128)(2,1)}), bf16[32,2,1,4096]{3,1,2,0:T(2,128)(2,1)S(1)}, u32[]{:S(2)}, u32[]{:S(2)}) async-start(bf16[32,2,1,4096]{3,1,2,0:T(2,128)(2,1)} %pad_maximum_fusion.3), calls=%async_computation.6 | async-start | bytes 1048576 | tf_op jit(solution)/shard_map/all_to_all | solution.py:129
  220.4 30.4 %collective-permute-start = (bf16[64,4096]{1,0:T(8,128)(2,1)S(1)}, bf16[64,4096]{1,0:T(8,128)(2,1)S(1)}, u32[]{:S(2)}, u32[]{:S(2)}) collective-permute-start(bf16[64,4096]{1,0:T(8,128)(2,1)S(1)} %copy-done.5), channel_id=1, source_target_pairs={{0,16},{16,32},{32,48},{48,64},{64,80},{80,96},{96,112},{112,128},... | collective-permute-start | bytes 1572872 | tf_op jit(solution)/shard_map/ppermute | solution.py:14
  222.4 34.8 %collective-permute-start.3 = (bf16[64,4096]{1,0:T(8,128)(2,1)}, bf16[64,4096]{1,0:T(8,128)(2,1)S(1)}, u32[]{:S(2)}, u32[]{:S(2)}) collective-permute-start(bf16[64,4096]{1,0:T(8,128)(2,1)} %collective-permute-done.2), channel_id=1, source_target_pairs={{0,16},{16,32},{32,48},{48,64},{64,80},{80,96},{96,112},{112,128},... | collective-permute-start | bytes 1572872 | tf_op jit(solution)/shard_map/ppermute | solution.py:14
  250.8 14.5 %collective-permute-start.1 = (bf16[64,4096]{1,0:T(8,128)(2,1)S(1)}, bf16[64,4096]{1,0:T(8,128)(2,1)S(1)}, u32[]{:S(2)}, u32[]{:S(2)}) collective-permute-start(bf16[64,4096]{1,0:T(8,128)(2,1)S(1)} %collective-permute-done), channel_id=1, source_target_pairs={{0,16},{16,32},{32,48},{48,64},{64,80},{80,96},{96,112},{112,128},... | collective-permute-start | bytes 1572872 | tf_op jit(solution)/shard_map/ppermute | solution.py:14
where the time goes:
time: 270 us; the launch traced here: 269 us
  waiting for transfers between devices  160 us (59%)
  starting transfers between devices  61.3 us (23%)
  matrix products  22.6 us (8%)
  local copies, waits for them, and re-layouts  19.4 us (7%)
  other arithmetic  4.32 us (2%)
    ppermute x4, waiting for transfers between devices, passed_along(): return lax.ppermute(shard, axis, pairs)  32.3 us
    all_to_all x1, waiting for transfers between devices, local(): lax.all_to_all(back_im, 'context', split_axis=1, concat_axis=0, tiled=True)  27.6 us
    all_to_all x1, waiting for transfers between devices, local(): lax.all_to_all(turned_re.reshape(span, 1, width_all), 'context', split_ax...  26.7 us
    all_to_all x1, waiting for transfers between devices, local(): lax.all_to_all(turned_im.reshape(span, 1, width_all), 'context', split_ax...  26.7 us
    all_to_all x1, waiting for transfers between devices, local(): lax.all_to_all(back_re, 'context', split_axis=1, concat_axis=0, tiled=True)  23.5 us
    all_to_all x1, waiting for transfers between devices, local(): lax.all_to_all(cyclic_form(hyena_in), 'context', split_axis=2, concat_axi...  16.1 us
    all_to_all x1, starting transfers between devices, local(): lax.all_to_all(cyclic_form(hyena_in), 'context', split_axis=2, concat_axi...  12.5 us
    ppermute x4, starting transfers between devices, passed_along(): return lax.ppermute(shard, axis, pairs)  10.3 us
  transfers between devices with their start and end apart: 11, of which 9 were waited for; matrix products, arithmetic and copies ran while one was open for 8% of the time, Pallas kernels for 0%

commit v1 on v0

v1 whole, which is shorter than its diff:
```python
import functools
import math

import jax
import jax.numpy as jnp
import ml_dtypes
import numpy as np
from jax import lax
from jax.experimental import pallas as pl
from jax.experimental.pallas import tpu as pltpu
from jax.sharding import PartitionSpec as P

HEAD_DIM = 128
BLOCK = 256
TILE = 128
VMEM_LIMIT = 48 * 1024 * 1024


def bf16_parts(table, count):
    parts = []
    rest = table.astype(np.float64)
    for _ in range(count):
        part = rest.astype(np.float32).astype(ml_dtypes.bfloat16)
        parts.append(part)
        rest = rest - part.astype(np.float64)
    return np.stack(parts)


def forward_table():
    freq = np.arange(BLOCK)[:, None] + 0.5
    angle = freq * np.arange(BLOCK)[None, :] * (math.pi / BLOCK)
    return np.concatenate([np.cos(angle), -np.sin(angle)], axis=0)


def inverse_table():
    freq = np.arange(BLOCK)[None, :] + 0.5
    angle = freq * (BLOCK + np.arange(BLOCK))[:, None] * (math.pi / BLOCK)
    return np.concatenate([np.cos(angle), -np.sin(angle)], axis=1) / BLOCK


def dot(left, right):
    return lax.dot_general(
        left, right, (((1,), (0,)), ((), ())), preferred_element_type=jnp.float32
    )


def pack_kernel(x_ref, k_ref, v_ref, out_ref):
    tok, width = x_ref.shape
    for head in range(width // HEAD_DIM):
        cols = slice(head * HEAD_DIM, (head + 1) * HEAD_DIM)
        for place, ref in enumerate((x_ref, k_ref, v_ref)):
            out_ref[head, place * tok : (place + 1) * tok, :] = ref[:, cols]


def filter_kernel(me_ref, filt_ref, table_ref, out_ref):
    blocks, _, _ = out_ref.shape
    tok = filt_ref.shape[2]
    per = BLOCK // tok
    me = me_ref[0]
    sign = 1.0 - 2.0 * (lax.broadcasted_iota(jnp.int32, (BLOCK, 1), 0) % 2).astype(jnp.float32)
    before_re = jnp.zeros((BLOCK, HEAD_DIM), jnp.float32)
    before_im = before_re
    for block in range(blocks):
        pieces = []
        for part in range(per):
            place = lax.bitwise_xor(me, jnp.int32(block * per + part))
            pieces.append(filt_ref[lax.bitwise_and(place, 1), lax.shift_right_logical(place, 1)])
        chunk = jnp.concatenate(pieces, axis=0)
        spec = dot(table_ref[0], chunk) + dot(table_ref[1], chunk)
        spec_re, spec_im = spec[:BLOCK], spec[BLOCK:]
        out_ref[block, :BLOCK, :] = before_re + sign * spec_im
        out_ref[block, BLOCK:, :] = before_im - sign * spec_re
        before_re, before_im = spec_re, spec_im


def main_kernel(y_ref, w_ref, fwd_ref, inv_ref, out_ref, spec, total_hi, total_lo, queries):
    sources, _, width = y_ref.shape
    tok = out_ref.shape[1]
    per = BLOCK // tok
    blocks = sources // per
    for pair in range(blocks // 2):
        both = jnp.concatenate(
            [
                y_ref[block * per : (block + 1) * per, :tok, :].reshape(BLOCK, width)
                for block in (2 * pair, 2 * pair + 1)
            ],
            axis=1,
        )
        got = dot(fwd_ref[0], both) + dot(fwd_ref[1], both)
        spec[2 * pair] = got[:, :width]
        spec[2 * pair + 1] = got[:, width:]

    def products(step, carry):
        low = pl.ds(pl.multiple_of(step * 8, 8), 8)
        high = pl.ds(pl.multiple_of(step * 8 + BLOCK, 8), 8)
        x_re = [spec[block, low, :] for block in range(blocks)]
        x_im = [spec[block, high, :] for block in range(blocks)]
        w_re = [w_ref[block, low, :] for block in range(blocks)]
        w_im = [w_ref[block, high, :] for block in range(blocks)]
        for block in range(blocks):
            re = im = None
            for first in range(block + 1):
                a, b = x_re[first], x_im[first]
                c, d = w_re[block - first], w_im[block - first]
                new_re, new_im = a * c - b * d, a * d + b * c
                re = new_re if re is None else re + new_re
                im = new_im if im is None else im + new_im
            spec[block, low, :] = re
            spec[block, high, :] = im
        return carry

    lax.fori_loop(0, BLOCK // 8, products, 0)
    for block in range(blocks):
        value = spec[block]
        hi = value.astype(jnp.bfloat16)
        cols = slice(block * width, (block + 1) * width)
        total_hi[:, cols] = hi
        total_lo[:, cols] = (value - hi.astype(jnp.float32)).astype(jnp.bfloat16)
    for pair in range(blocks // 2):
        cols = slice(2 * pair * width, (2 * pair + 2) * width)
        hi, lo = total_hi[:, cols], total_lo[:, cols]
        conv = dot(inv_ref[0], hi) + (dot(inv_ref[0], lo) + dot(inv_ref[1], hi))
        conv = conv.astype(jnp.bfloat16)
        queries[2 * pair * BLOCK : (2 * pair + 1) * BLOCK, :] = conv[:, :width]
        queries[(2 * pair + 1) * BLOCK : (2 * pair + 2) * BLOCK, :] = conv[:, width:]

    reach = TILE // tok
    factor = math.log2(math.e) / math.sqrt(HEAD_DIM)
    for tile in range(sources // reach):
        first = max(tile * reach - reach, 0)
        last = (tile + 1) * reach
        span = (last - first) * tok
        ahead = tile * TILE - first * tok
        key = y_ref[first:last, tok : 2 * tok, :].reshape(span, width)
        val = y_ref[first:last, 2 * tok : 3 * tok, :].reshape(span, width)
        query = queries[tile * TILE : (tile + 1) * TILE, :]
        scores = lax.dot_general(
            query, key, (((1,), (1,)), ((), ())), preferred_element_type=jnp.float32
        )
        row = lax.broadcasted_iota(jnp.int32, (TILE, span), 0)
        col = lax.broadcasted_iota(jnp.int32, (TILE, span), 1)
        allowed = (col <= row + ahead) & (col >= row // tok * tok + ahead - 2 * tok)
        scores = jnp.where(allowed, scores, -1e30)
        top = jnp.max(scores, axis=-1, keepdims=True)
        expo = jnp.exp2((scores - top) * factor)
        probs = (expo * (1.0 / jnp.sum(expo, axis=-1, keepdims=True))).astype(jnp.bfloat16)
        mixed = dot(probs, val).astype(jnp.bfloat16)
        out_ref[tile * reach : last] = mixed.reshape(reach, tok, width)


def gather_filt(filt):
    held = filt[None]
    peers = lax.axis_size("context")
    bit = 2
    while bit < peers:
        other = lax.ppermute(held, "context", [(i, i ^ bit) for i in range(peers)])
        held = jnp.concatenate([held, other], axis=0)
        bit *= 2
    other = lax.ppermute(held, "context", [(i, i ^ 1) for i in range(peers)])
    return jnp.stack([held, other])


def vmem(count):
    return [pl.BlockSpec(memory_space=pltpu.VMEM)] * count


def local(hyena_in, filt, keys, values):
    peers = lax.axis_size("context")
    tok, width = hyena_in.shape
    blocks = peers * tok // BLOCK
    params = pltpu.CompilerParams(vmem_limit_bytes=VMEM_LIMIT)
    fwd = jnp.asarray(bf16_parts(forward_table(), 2))
    inv = jnp.asarray(bf16_parts(inverse_table(), 2))
    me = lax.axis_index("context").astype(jnp.int32).reshape(1)

    packed = pl.pallas_call(
        pack_kernel,
        out_shape=jax.ShapeDtypeStruct((peers, 3 * tok, HEAD_DIM), jnp.bfloat16),
        in_specs=vmem(3),
        out_specs=vmem(1)[0],
        compiler_params=params,
        cost_estimate=pl.CostEstimate(flops=0, bytes_accessed=6 * tok * width * 2, transcendentals=0),
        name="pack",
    )(hyena_in, keys, values)
    moved = lax.all_to_all(packed, "context", split_axis=0, concat_axis=0, tiled=True)

    all_filt = gather_filt(filt)
    spectra = pl.pallas_call(
        filter_kernel,
        out_shape=jax.ShapeDtypeStruct((blocks, 2 * BLOCK, HEAD_DIM), jnp.float32),
        in_specs=[pl.BlockSpec(memory_space=pltpu.SMEM)] + vmem(2),
        out_specs=vmem(1)[0],
        compiler_params=params,
        cost_estimate=pl.CostEstimate(
            flops=blocks * 8 * BLOCK * BLOCK * HEAD_DIM, bytes_accessed=4 << 20, transcendentals=0
        ),
        name="filter_spectra",
    )(me, all_filt, fwd)

    mixed = pl.pallas_call(
        main_kernel,
        out_shape=jax.ShapeDtypeStruct((peers, tok, HEAD_DIM), jnp.bfloat16),
        in_specs=vmem(4),
        out_specs=vmem(1)[0],
        scratch_shapes=[
            pltpu.VMEM((blocks, 2 * BLOCK, HEAD_DIM), jnp.float32),
            pltpu.VMEM((2 * BLOCK, blocks * HEAD_DIM), jnp.bfloat16),
            pltpu.VMEM((2 * BLOCK, blocks * HEAD_DIM), jnp.bfloat16),
            pltpu.VMEM((peers * tok, HEAD_DIM), jnp.bfloat16),
        ],
        compiler_params=params,
        cost_estimate=pl.CostEstimate(flops=4 << 30, bytes_accessed=5 << 20, transcendentals=1 << 19),
        name="conv_attention",
    )(moved, spectra, fwd, inv)
    home = lax.all_to_all(mixed, "context", split_axis=0, concat_axis=0, tiled=True)
    return home.transpose(1, 0, 2).reshape(tok, width)


def solution(mesh):
    spec = P(("dp", "context"), None)
    return jax.shard_map(
        local, mesh=mesh, in_specs=(spec,) * 4, out_specs=spec, check_vma=False
    )
```

time: 270 us -> 119 us (0.44)
  the two profiles are of different devices: /device:TPU:126 before, /device:TPU:1 now
where the time goes in v1:
time: 119 us; the launch traced here: 118 us
  starting transfers between devices  44.9 us (38%)
  waiting for transfers between devices  32.9 us (28%)
  blocking collectives  27.4 us (23%)
  Pallas kernels  8.79 us (7%)
  local copies, waits for them, and re-layouts  4.06 us (3%)
    ppermute x4, waiting for transfers between devices, gather_filt(): other = lax.ppermute(held, 'context', [(i, i ^ bit) for i in range(peers)])  31.8 us
    all_to_all x1, blocking collectives, local(): lax.all_to_all(mixed, 'context', split_axis=0, concat_axis=0, tiled=True)  27.4 us
    ppermute x4, starting transfers between devices, gather_filt(): other = lax.ppermute(held, 'context', [(i, i ^ bit) for i in range(peers)])  21.3 us
    all_to_all x1, starting transfers between devices, local(): lax.all_to_all(packed, 'context', split_axis=0, concat_axis=0, tiled=True)  14.6 us
    ppermute x1, starting transfers between devices, gather_filt(): other = lax.ppermute(held, 'context', [(i, i ^ 1) for i in range(peers)])  9 us
    pallas_call x1, Pallas kernels, local(): pl.pallas_call(main_kernel, out_shape=jax.ShapeDtypeStruct((peers, tok, H...  6.09 us
    unnamed x16, local copies, waits for them, and re-layouts  3.18 us
  transfers between devices with their start and end apart: 6, of which 5 were waited for; matrix products, arithmetic and copies ran while one was open for 0% of the time, Pallas kernels for 1%

profile of v1, /device:TPU:1, one launch (start us, length us, event | category | flops | bytes accessed | tf_op | source)
XLA Modules:
  0.0 118.4 jit_solution(15526999218392320376)
XLA Ops:
  0.0 0.0 copy-start
  0.0 1.0 copy-done
  1.0 0.0 copy-start.1
  1.0 1.0 copy-done.1
  2.1 0.0 copy-start.2
  2.1 1.0 copy-done.2
  3.1 1.4 %pack.1 = bf16[32,192,128]{2,1,0:T(8,128)(2,1)} custom-call(bf16[64,4096]{1,0:T(8,128)(2,1)S(1)} %copy-done, bf16[64,4096]{1,0:T(8,128)(2,1)S(1)} %copy-done.1, bf16[64,4096]{1,0:T(8,128)(2,1)S(1)} %copy-done.2), custom_call_target="tpu_custom_call" | custom-call | bytes 3145728 | tf_op jit(solution)/shard_map/pack/pallas_call | solution.py:176
  4.5 0.0 copy-start.5
  4.6 14.6 %all-to-all-start = ((bf16[32,192,128]{2,1,0:T(8,128)(2,1)}), bf16[32,192,128]{2,1,0:T(8,128)(2,1)}, u32[]{:S(2)}, u32[]{:S(2)}) async-start(bf16[32,192,128]{2,1,0:T(8,128)(2,1)} %pack.1), calls=%async_computation | async-start | bytes 3145728 | tf_op jit(solution)/shard_map/all_to_all | solution.py:185
  19.2 0.0 copy-start.3
  19.2 0.0 copy-done.5
  19.2 4.3 %collective-permute-start = (bf16[1,64,128]{2,1,0:T(8,128)(2,1)S(1)}, bf16[1,64,128]{2,1,0:T(8,128)(2,1)S(1)}, u32[]{:S(2)}, u32[]{:S(2)}) collective-permute-start(bf16[1,64,128]{2,1,0:T(8,128)(2,1)S(1)} %bitcast.12), channel_id=1, source_target_pairs={{0,32},{16,48},{32,0},{48,16},{64,96},{80,112},{96,64},{112,80},{1... | collective-permute-start | bytes 49160 | tf_op jit(solution)/shard_map/ppermute | solution.py:156
  23.5 20.5 %collective-permute-done = bf16[1,64,128]{2,1,0:T(8,128)(2,1)S(1)} collective-permute-done((bf16[1,64,128]{2,1,0:T(8,128)(2,1)S(1)}, bf16[1,64,128]{2,1,0:T(8,128)(2,1)S(1)}, u32[]{:S(2)}, u32[]{:S(2)}) %collective-permute-start) | collective-permute-done | bytes 16416 | tf_op jit(solution)/shard_map/ppermute | solution.py:156
  44.1 9.3 %collective-permute-start.1 = (bf16[2,64,128]{2,1,0:T(8,128)(2,1)S(1)}, bf16[2,64,128]{2,1,0:T(8,128)(2,1)S(1)}, u32[]{:S(2)}, u32[]{:S(2)}) collective-permute-start(bf16[2,64,128]{2,1,0:T(8,128)(2,1)S(1)} %pad_maximum_fusion.3), channel_id=1, source_target_pairs={{0,64},{16,80},{32,96},{48,112},{64,0},{80,16},{96,32},{112,48},{1... | collective-permute-start | bytes 98312 | tf_op jit(solution)/shard_map/ppermute | solution.py:156
  53.4 6.5 %collective-permute-done.1 = bf16[2,64,128]{2,1,0:T(8,128)(2,1)S(1)} collective-permute-done((bf16[2,64,128]{2,1,0:T(8,128)(2,1)S(1)}, bf16[2,64,128]{2,1,0:T(8,128)(2,1)S(1)}, u32[]{:S(2)}, u32[]{:S(2)}) %collective-permute-start.1) | collective-permute-done | bytes 32800 | tf_op jit(solution)/shard_map/ppermute | solution.py:156
  60.0 3.1 %collective-permute-start.2 = (bf16[4,64,128]{2,1,0:T(8,128)(2,1)S(1)}, bf16[4,64,128]{2,1,0:T(8,128)(2,1)S(1)}, u32[]{:S(2)}, u32[]{:S(2)}) collective-permute-start(bf16[4,64,128]{2,1,0:T(8,128)(2,1)S(1)} %pad_maximum_fusion.2), channel_id=1, source_target_pairs={{0,128},{16,144},{32,160},{48,176},{64,192},{80,208},{96,224},{112... | collective-permute-start | bytes 196616 | tf_op jit(solution)/shard_map/ppermute | solution.py:156
  63.1 1.9 %collective-permute-done.2 = bf16[4,64,128]{2,1,0:T(8,128)(2,1)S(1)} collective-permute-done((bf16[4,64,128]{2,1,0:T(8,128)(2,1)S(1)}, bf16[4,64,128]{2,1,0:T(8,128)(2,1)S(1)}, u32[]{:S(2)}, u32[]{:S(2)}) %collective-permute-start.2) | collective-permute-done | bytes 65568 | tf_op jit(solution)/shard_map/ppermute | solution.py:156
  65.0 4.5 %collective-permute-start.3 = (bf16[8,64,128]{2,1,0:T(8,128)(2,1)S(1)}, bf16[8,64,128]{2,1,0:T(8,128)(2,1)S(1)}, u32[]{:S(2)}, u32[]{:S(2)}) collective-permute-start(bf16[8,64,128]{2,1,0:T(8,128)(2,1)S(1)} %pad_maximum_fusion.1), channel_id=1, source_target_pairs={{0,256},{16,272},{32,288},{48,304},{64,320},{80,336},{96,352},{112... | collective-permute-start | bytes 393224 | tf_op jit(solution)/shard_map/ppermute | solution.py:156
  69.6 2.9 %collective-permute-done.3 = bf16[8,64,128]{2,1,0:T(8,128)(2,1)S(1)} collective-permute-done((bf16[8,64,128]{2,1,0:T(8,128)(2,1)S(1)}, bf16[8,64,128]{2,1,0:T(8,128)(2,1)S(1)}, u32[]{:S(2)}, u32[]{:S(2)}) %collective-permute-start.3) | collective-permute-done | bytes 131104 | tf_op jit(solution)/shard_map/ppermute | solution.py:156
  72.5 9.0 %collective-permute-start.4 = (bf16[16,64,128]{2,1,0:T(8,128)(2,1)S(1)}, bf16[16,64,128]{2,1,0:T(8,128)(2,1)S(1)}, u32[]{:S(2)}, u32[]{:S(2)}) collective-permute-start(bf16[16,64,128]{2,1,0:T(8,128)(2,1)S(1)} %constant_dynamic-update-slice_fusion), channel_id=1, source_target_pairs={{0,16},{16,0},{32,48},{48,32},{64,80},{80,64},{96,112},{112,96},{1... | collective-permute-start | bytes 786440 | tf_op jit(solution)/shard_map/ppermute | solution.py:159
  81.5 1.1 collective-permute-done.4
  82.6 0.1 pad_maximum_fusion.filt_ref
  82.7 0.0 copy-done.3
  82.7 0.0 copy-start.4
  82.7 1.3 %filter_spectra.1.w_ref = f32[8,512,128]{2,1,0:T(8,128)S(1)} custom-call(s32[1]{0:T(128)} %bitcast.me_ref, bf16[2,16,64,128]{3,2,1,0:T(8,128)(2,1)S(1)} %pad_maximum_fusion.filt_ref, bf16[2,512,256]{2,1,0:T(8,128)(2,1)S(1)} %copy-done.3), custom_call_target="tpu_custom_call" | custom-call | flops 536870912 | bytes 4194304 | tf_op jit(solution)/shard_map/filter_spectra/pallas_call | solution.py:188
  84.0 0.0 all-to-all-done.y_ref
  84.0 0.0 copy-done.4
  84.0 6.1 %conv_attention.1 = bf16[32,64,128]{2,1,0:T(8,128)(2,1)S(1)} custom-call(bf16[32,192,128]{2,1,0:T(8,128)(2,1)} %all-to-all-done.y_ref, f32[8,512,128]{2,1,0:T(8,128)S(1)} %filter_spectra.1.w_ref, bf16[2,512,256]{2,1,0:T(8,128)(2,1)S(1)} %copy-done.3, bf16[2,256,512]{2,1,0:T(8,128)(2,1)S(1)} %copy-done.4), custom_call_target="tpu_custom_call" | custom-call | flops 4294967296 | bytes 5242880 | tf_op jit(solution)/shard_map/conv_attention/pallas_call | solution.py:200
  90.1 27.4 %all_to_all.10 = bf16[32,64,128]{2,1,0:T(8,128)(2,1)S(1)} all-to-all(bf16[32,64,128]{2,1,0:T(8,128)(2,1)S(1)} %conv_attention.1), channel_id=1, replica_groups=mesh['context'=32,'dp'=16] {'context'}, dimensions={0} | all-to-all | bytes 1048576 | tf_op jit(solution)/shard_map/all_to_all | solution.py:215
  117.5 0.9 copy_bitcast_fusion
  (8 shorter events, 0.1 us)
Async XLA Ops:
  0.0 1.0 copy-start
  1.0 1.0 copy-start.1
  2.1 1.0 copy-start.2
  4.5 14.6 %copy-start.5 = (bf16[64,128]{1,0:T(8,128)(2,1)S(1)}, bf16[64,128]{1,0:T(8,128)(2,1)}, u32[]{:S(2)}) copy-start(bf16[64,128]{1,0:T(8,128)(2,1)} %param.7) | copy-start | bytes 49156
  4.6 79.4 %all-to-all-start = ((bf16[32,192,128]{2,1,0:T(8,128)(2,1)}), bf16[32,192,128]{2,1,0:T(8,128)(2,1)}, u32[]{:S(2)}, u32[]{:S(2)}) async-start(bf16[32,192,128]{2,1,0:T(8,128)(2,1)} %pack.1), calls=%async_computation | async-start | bytes 3145728 | tf_op jit(solution)/shard_map/all_to_all | solution.py:185
  19.2 63.5 %copy-start.3 = (bf16[2,512,256]{2,1,0:T(8,128)(2,1)S(1)}, bf16[2,512,256]{2,1,0:T(8,128)(2,1)}, u32[]{:S(2)}) copy-start(bf16[2,512,256]{2,1,0:T(8,128)(2,1)} %constant.10.clone.table_ref.fwd_ref) | copy-start | bytes 1572868
  19.2 24.9 %collective-permute-start = (bf16[1,64,128]{2,1,0:T(8,128)(2,1)S(1)}, bf16[1,64,128]{2,1,0:T(8,128)(2,1)S(1)}, u32[]{:S(2)}, u32[]{:S(2)}) collective-permute-start(bf16[1,64,128]{2,1,0:T(8,128)(2,1)S(1)} %bitcast.12), channel_id=1, source_target_pairs={{0,32},{16,48},{32,0},{48,16},{64,96},{80,112},{96,64},{112,80},{1... | collective-permute-start | bytes 49160 | tf_op jit(solution)/shard_map/ppermute | solution.py:156
  44.1 15.9 %collective-permute-start.1 = (bf16[2,64,128]{2,1,0:T(8,128)(2,1)S(1)}, bf16[2,64,128]{2,1,0:T(8,128)(2,1)S(1)}, u32[]{:S(2)}, u32[]{:S(2)}) collective-permute-start(bf16[2,64,128]{2,1,0:T(8,128)(2,1)S(1)} %pad_maximum_fusion.3), channel_id=1, source_target_pairs={{0,64},{16,80},{32,96},{48,112},{64,0},{80,16},{96,32},{112,48},{1... | collective-permute-start | bytes 98312 | tf_op jit(solution)/shard_map/ppermute | solution.py:156
  60.0 5.0 %collective-permute-start.2 = (bf16[4,64,128]{2,1,0:T(8,128)(2,1)S(1)}, bf16[4,64,128]{2,1,0:T(8,128)(2,1)S(1)}, u32[]{:S(2)}, u32[]{:S(2)}) collective-permute-start(bf16[4,64,128]{2,1,0:T(8,128)(2,1)S(1)} %pad_maximum_fusion.2), channel_id=1, source_target_pairs={{0,128},{16,144},{32,160},{48,176},{64,192},{80,208},{96,224},{112... | collective-permute-start | bytes 196616 | tf_op jit(solution)/shard_map/ppermute | solution.py:156
  65.0 7.5 %collective-permute-start.3 = (bf16[8,64,128]{2,1,0:T(8,128)(2,1)S(1)}, bf16[8,64,128]{2,1,0:T(8,128)(2,1)S(1)}, u32[]{:S(2)}, u32[]{:S(2)}) collective-permute-start(bf16[8,64,128]{2,1,0:T(8,128)(2,1)S(1)} %pad_maximum_fusion.1), channel_id=1, source_target_pairs={{0,256},{16,272},{32,288},{48,304},{64,320},{80,336},{96,352},{112... | collective-permute-start | bytes 393224 | tf_op jit(solution)/shard_map/ppermute | solution.py:156
  72.5 10.1 %collective-permute-start.4 = (bf16[16,64,128]{2,1,0:T(8,128)(2,1)S(1)}, bf16[16,64,128]{2,1,0:T(8,128)(2,1)S(1)}, u32[]{:S(2)}, u32[]{:S(2)}) collective-permute-start(bf16[16,64,128]{2,1,0:T(8,128)(2,1)S(1)} %constant_dynamic-update-slice_fusion), channel_id=1, source_target_pairs={{0,16},{16,0},{32,48},{48,32},{64,80},{80,64},{96,112},{112,96},{1... | collective-permute-start | bytes 786440 | tf_op jit(solution)/shard_map/ppermute | solution.py:159
  82.7 1.3 %copy-start.4 = (bf16[2,256,512]{2,1,0:T(8,128)(2,1)S(1)}, bf16[2,256,512]{2,1,0:T(8,128)(2,1)}, u32[]{:S(2)}) copy-start(bf16[2,256,512]{2,1,0:T(8,128)(2,1)} %constant.11.clone.inv_ref) | copy-start | bytes 1572868

commit v2 on v1

v2 whole, which is shorter than its diff:
```python
import math

import jax
import jax.numpy as jnp
import ml_dtypes
import numpy as np
from jax import lax
from jax.experimental import pallas as pl
from jax.experimental.pallas import tpu as pltpu
from jax.sharding import PartitionSpec as P

HEAD_DIM = 128
BLOCK = 256
TILE = 128
VMEM_LIMIT = 48 * 1024 * 1024
CHUNKS = 4


def bf16_parts(table, count):
    parts = []
    rest = table.astype(np.float64)
    for _ in range(count):
        part = rest.astype(np.float32).astype(ml_dtypes.bfloat16)
        parts.append(part)
        rest = rest - part.astype(np.float64)
    return np.stack(parts)


def forward_table():
    freq = np.arange(BLOCK)[:, None] + 0.5
    angle = freq * np.arange(BLOCK)[None, :] * (math.pi / BLOCK)
    return np.concatenate([np.cos(angle), -np.sin(angle)], axis=0)


def inverse_table():
    freq = np.arange(BLOCK)[None, :] + 0.5
    angle = freq * (BLOCK + np.arange(BLOCK))[:, None] * (math.pi / BLOCK)
    return np.concatenate([np.cos(angle), -np.sin(angle)], axis=1) / BLOCK


def dot(left, right):
    return lax.dot_general(
        left, right, (((1,), (0,)), ((), ())), preferred_element_type=jnp.float32
    )


def copy(src, dst, sem):
    return pltpu.make_async_copy(src, dst, sem)


def pack_kernel(x_ref, k_ref, v_ref, f_ref, out_ref, held, half, load, store):
    tok, width = x_ref.shape
    heads = width // HEAD_DIM
    group = heads // CHUNKS
    part = tok // 2
    filters = copy(f_ref, half, load.at[CHUNKS])
    filters.start()
    loads = [[] for _ in range(CHUNKS)]
    for head in range(heads):
        cols = pl.ds(head * HEAD_DIM, HEAD_DIM)
        for place, ref in enumerate((x_ref, k_ref, v_ref)):
            step = copy(
                ref.at[:, cols], held.at[head, pl.ds(place * tok, tok)], load.at[head // group]
            )
            step.start()
            loads[head // group].append(step)
    filters.wait()
    for head in range(heads):
        first = head % 2 * part
        held[head, 3 * tok :, :] = half[first : first + part, :]
    stores = []
    for chunk in range(CHUNKS):
        for step in loads[chunk]:
            step.wait()
        some = pl.ds(chunk * group, group)
        step = copy(held.at[some], out_ref.at[some], store.at[chunk])
        step.start()
        stores.append(step)
    for step in stores:
        step.wait()


def pack(hyena_in, keys, values, filt):
    tok, width = hyena_in.shape
    heads = width // HEAD_DIM
    shape = (heads, 3 * tok + tok // 2, HEAD_DIM)
    anywhere = pl.BlockSpec(memory_space=pl.ANY)
    return pl.pallas_call(
        pack_kernel,
        out_shape=jax.ShapeDtypeStruct(shape, jnp.bfloat16),
        in_specs=[anywhere] * 4,
        out_specs=anywhere,
        scratch_shapes=[
            pltpu.VMEM(shape, jnp.bfloat16),
            pltpu.VMEM((tok, HEAD_DIM), jnp.bfloat16),
            pltpu.SemaphoreType.DMA((CHUNKS + 1,)),
            pltpu.SemaphoreType.DMA((CHUNKS,)),
        ],
        cost_estimate=pl.CostEstimate(
            flops=0, bytes_accessed=14 * tok * width, transcendentals=0
        ),
        name="pack",
    )(hyena_in, keys, values, filt)


def main_kernel(
    me_ref, y_ref, other_ref, fwd_ref, inv_ref, out_ref, spec, fspec, filt, bias, queries
):
    sources, _, width = y_ref.shape
    tok = out_ref.shape[1]
    half = tok // 2
    per = BLOCK // tok
    blocks = sources // per
    odd = lax.bitwise_and(me_ref[0], 1)
    for source in range(sources):
        at = pl.multiple_of(source * tok + odd * half, half)
        filt[pl.ds(at, half), :] = y_ref[source, 3 * tok : 3 * tok + half, :]
        at = pl.multiple_of(source * tok + (1 - odd) * half, half)
        filt[pl.ds(at, half), :] = other_ref[source]

    for pair in range(blocks // 2):
        x_both = jnp.concatenate(
            [
                y_ref[block * per : (block + 1) * per, :tok, :].reshape(BLOCK, width)
                for block in (2 * pair, 2 * pair + 1)
            ],
            axis=1,
        )
        f_both = jnp.concatenate(
            [
                filt[block * BLOCK : (block + 1) * BLOCK, :]
                for block in (2 * pair, 2 * pair + 1)
            ],
            axis=1,
        )
        for both, result in ((x_both, spec), (f_both, fspec)):
            got = dot(fwd_ref[0], both) + dot(fwd_ref[1], both)
            result[2 * pair] = got[:, :width]
            result[2 * pair + 1] = got[:, width:]

    sign = 1.0 - 2.0 * (lax.broadcasted_iota(jnp.int32, (8, width), 0) % 2).astype(jnp.float32)

    def products(step, carry):
        low = pl.ds(pl.multiple_of(step * 8, 8), 8)
        high = pl.ds(pl.multiple_of(step * 8 + BLOCK, 8), 8)
        x_re = [spec[block, low, :] for block in range(blocks)]
        x_im = [spec[block, high, :] for block in range(blocks)]
        x_sum = [re + im for re, im in zip(x_re, x_im)]
        f_re = [fspec[block, low, :] for block in range(blocks)]
        f_im = [fspec[block, high, :] for block in range(blocks)]
        w_re, w_im = [], []
        for block in range(blocks):
            re, im = sign * f_im[block], -sign * f_re[block]
            w_re.append(re + f_re[block - 1] if block else re)
            w_im.append(im + f_im[block - 1] if block else im)
        w_sum = [re + im for re, im in zip(w_re, w_im)]
        for block in range(blocks):
            p = q = r = None
            for first in range(block + 1):
                other = block - first
                p_new = x_re[first] * w_re[other]
                q_new = x_im[first] * w_im[other]
                r_new = x_sum[first] * w_sum[other]
                p = p_new if p is None else p + p_new
                q = q_new if q is None else q + q_new
                r = r_new if r is None else r + r_new
            spec[block, low, :] = p - q
            spec[block, high, :] = r - (p + q)
        return carry

    lax.fori_loop(0, BLOCK // 8, products, 0, unroll=4)
    for pair in range(blocks // 2):
        value = jnp.concatenate([spec[2 * pair], spec[2 * pair + 1]], axis=1)
        hi = value.astype(jnp.bfloat16)
        lo = (value - hi.astype(jnp.float32)).astype(jnp.bfloat16)
        conv = dot(inv_ref[0], hi) + (dot(inv_ref[0], lo) + dot(inv_ref[1], hi))
        conv = conv.astype(jnp.bfloat16)
        queries[2 * pair * BLOCK : (2 * pair + 1) * BLOCK, :] = conv[:, :width]
        queries[(2 * pair + 1) * BLOCK : (2 * pair + 2) * BLOCK, :] = conv[:, width:]

    reach = TILE // tok
    factor = math.log2(math.e) / math.sqrt(HEAD_DIM)
    row = lax.broadcasted_iota(jnp.int32, (TILE, 2 * TILE), 0)
    col = lax.broadcasted_iota(jnp.int32, (TILE, 2 * TILE), 1)
    allowed = (col <= row + TILE) & (col >= row // tok * tok)
    bias[...] = jnp.where(allowed, 0.0, -1e30)
    for tile in range(sources // reach):
        first = max(tile * reach - reach, 0)
        last = (tile + 1) * reach
        span = (last - first) * tok
        key = y_ref[first:last, tok : 2 * tok, :].reshape(span, width)
        val = y_ref[first:last, 2 * tok : 3 * tok, :].reshape(span, width)
        query = queries[tile * TILE : (tile + 1) * TILE, :]
        scores = lax.dot_general(
            query, key, (((1,), (1,)), ((), ())), preferred_element_type=jnp.float32
        )
        scores = scores + bias[:, 2 * TILE - span :]
        top = jnp.max(scores, axis=-1, keepdims=True)
        expo = jnp.exp2((scores - top) * factor)
        probs = (expo * (1.0 / jnp.sum(expo, axis=-1, keepdims=True))).astype(jnp.bfloat16)
        mixed = dot(probs, val).astype(jnp.bfloat16)
        out_ref[tile * reach : last] = mixed.reshape(reach, tok, width)


def vmem(count):
    return [pl.BlockSpec(memory_space=pltpu.VMEM)] * count


def local(hyena_in, filt, keys, values):
    peers = lax.axis_size("context")
    tok, width = hyena_in.shape
    blocks = peers * tok // BLOCK
    fwd = jnp.asarray(bf16_parts(forward_table(), 2))
    inv = jnp.asarray(bf16_parts(inverse_table(), 2))
    me = lax.axis_index("context").astype(jnp.int32).reshape(1)

    packed = pack(hyena_in, keys, values, filt)
    moved = lax.all_to_all(packed, "context", split_axis=0, concat_axis=0, tiled=True)
    other = lax.ppermute(moved[:, 3 * tok :], "context", [(i, i ^ 1) for i in range(peers)])

    mixed = pl.pallas_call(
        main_kernel,
        out_shape=jax.ShapeDtypeStruct((peers, tok, HEAD_DIM), jnp.bfloat16),
        in_specs=[pl.BlockSpec(memory_space=pltpu.SMEM)] + vmem(4),
        out_specs=vmem(1)[0],
        scratch_shapes=[
            pltpu.VMEM((blocks, 2 * BLOCK, HEAD_DIM), jnp.float32),
            pltpu.VMEM((blocks, 2 * BLOCK, HEAD_DIM), jnp.float32),
            pltpu.VMEM((peers * tok, HEAD_DIM), jnp.bfloat16),
            pltpu.VMEM((TILE, 2 * TILE), jnp.float32),
            pltpu.VMEM((peers * tok, HEAD_DIM), jnp.bfloat16),
        ],
        compiler_params=pltpu.CompilerParams(vmem_limit_bytes=VMEM_LIMIT),
        cost_estimate=pl.CostEstimate(flops=5 << 30, bytes_accessed=5 << 20, transcendentals=1 << 19),
        name="conv_attention",
    )(me, moved, other, fwd, inv)
    home = lax.all_to_all(mixed, "context", split_axis=0, concat_axis=0, tiled=True)
    return home.transpose(1, 0, 2).reshape(tok, width)


def solution(mesh):
    spec = P(("dp", "context"), None)
    return jax.shard_map(
        local, mesh=mesh, in_specs=(spec,) * 4, out_specs=spec, check_vma=False
    )
```

time: 119 us -> 93.5 us (0.79)
  blocking collectives: 27.4 us -> 81.2 us
  starting transfers between devices: 44.9 us -> 2.31 us
  waiting for transfers between devices: 32.9 us -> 1.14 us
  local copies, waits for them, and re-layouts: 4.06 us -> 0.89 us
  Pallas kernels: 8.79 us -> 7.1 us
    all_to_all x0 -> x1, blocking collectives: none -> 52.6 us  [local(): lax.all_to_all(packed, 'context', split_axis=0, concat_axis=0, tiled=True)]
    ppermute x5 -> x1, waiting for transfers between devices: 32.9 us -> 1.14 us  [local(): lax.ppermute(moved[:, 3 * tok:], 'context', [(i, i ^ 1) for i in range(pe...]
    ppermute x5 -> x1, starting transfers between devices: 30.3 us -> 2.31 us  [local(): lax.ppermute(moved[:, 3 * tok:], 'context', [(i, i ^ 1) for i in range(pe...]
    all_to_all x1 -> x0, starting transfers between devices: 14.6 us -> none  [local(): lax.all_to_all(packed, 'context', split_axis=0, concat_axis=0, tiled=True)]
    unnamed x16 -> x4, local copies, waits for them, and re-layouts: 3.18 us -> 0.01 us
    pallas_call x1, Pallas kernels: 6.09 us -> 4.82 us  [local(): pl.pallas_call(main_kernel, out_shape=jax.ShapeDtypeStruct((peers, tok, H...]
    pallas_call x2 -> x1, Pallas kernels: 2.69 us -> 2.28 us  [pack(): pl.pallas_call(pack_kernel, out_shape=jax.ShapeDtypeStruct(shape, jnp.bfl...]
  transfers between devices with their start and end apart: 6 -> 1, of which waited for: 5 -> 1; matrix products, arithmetic and copies ran while one was open for 0% -> 0% of each run, Pallas kernels for 1% -> 0%
where the time goes in v2:
time: 93.5 us; the launch traced here: 92.7 us
  blocking collectives  81.2 us (87%)
  Pallas kernels  7.1 us (8%)
  starting transfers between devices  2.31 us (2%)
  waiting for transfers between devices  1.14 us (1%)
    all_to_all x1, blocking collectives, local(): lax.all_to_all(packed, 'context', split_axis=0, concat_axis=0, tiled=True)  52.6 us
    all_to_all x1, blocking collectives, local(): lax.all_to_all(mixed, 'context', split_axis=0, concat_axis=0, tiled=True)  28.6 us
    pallas_call x1, Pallas kernels, local(): pl.pallas_call(main_kernel, out_shape=jax.ShapeDtypeStruct((peers, tok, H...  4.82 us
    ppermute x1, starting transfers between devices, local(): lax.ppermute(moved[:, 3 * tok:], 'context', [(i, i ^ 1) for i in range(pe...  2.31 us
    pallas_call x1, Pallas kernels, pack(): pl.pallas_call(pack_kernel, out_shape=jax.ShapeDtypeStruct(shape, jnp.bfl...  2.28 us
  transfers between devices with their start and end apart: 1, of which 1 were waited for; matrix products, arithmetic and copies ran while one was open for 0% of the time, Pallas kernels for 0%

profile of v2, /device:TPU:1, one launch (start us, length us, event | category | flops | bytes accessed | tf_op | source)
XLA Modules:
  0.0 92.7 jit_solution(11690297137047528188)
XLA Ops:
  0.0 2.3 %pack.1 = bf16[32,224,128]{2,1,0:T(8,128)(2,1)} custom-call(bf16[64,4096]{1,0:T(8,128)(2,1)} %x_ref.1, bf16[64,4096]{1,0:T(8,128)(2,1)} %k_ref.1, bf16[64,4096]{1,0:T(8,128)(2,1)} %v_ref.1, bf16[64,128]{1,0:T(8,128)(2,1)} %f_ref.1), custom_call_target="tpu_custom_call" | custom-call | bytes 3670016 | tf_op jit(solution)/shard_map/pack/pallas_call | solution.py:88
  2.3 0.0 copy-start
  2.3 0.0 copy-start.1
  2.3 52.6 %all_to_all.10.y_ref = bf16[32,224,128]{2,1,0:T(8,128)(2,1)S(1)} all-to-all(bf16[32,224,128]{2,1,0:T(8,128)(2,1)} %pack.1), channel_id=1, replica_groups=mesh['context'=32,'dp'=16] {'context'}, dimensions={0} | all-to-all | bytes 3670016 | tf_op jit(solution)/shard_map/all_to_all | solution.py:218
  55.0 2.3 %collective-permute-start = (bf16[32,32,128]{2,1,0:T(8,128)(2,1)S(1)}, bf16[32,32,128]{2,1,0:T(8,128)(2,1)S(1)}, u32[]{:S(2)}, u32[]{:S(2)}) collective-permute-start(bf16[32,32,128]{2,1,0:T(8,128)(2,1)S(1)} %slice.4), channel_id=1, source_target_pairs={{0,16},{16,0},{32,48},{48,32},{64,80},{80,64},{96,112},{112,96},{1... | collective-permute-start | bytes 786440 | tf_op jit(solution)/shard_map/ppermute | solution.py:219
  57.3 1.1 %collective-permute-done.other_ref = bf16[32,32,128]{2,1,0:T(8,128)(2,1)S(1)} collective-permute-done((bf16[32,32,128]{2,1,0:T(8,128)(2,1)S(1)}, bf16[32,32,128]{2,1,0:T(8,128)(2,1)S(1)}, u32[]{:S(2)}, u32[]{:S(2)}) %collective-permute-start) | collective-permute-done | bytes 262176 | tf_op jit(solution)/shard_map/ppermute | solution.py:219
  58.4 0.0 copy-done
  58.4 0.0 copy-done.1
  58.4 4.8 %conv_attention.1 = bf16[32,64,128]{2,1,0:T(8,128)(2,1)S(1)} custom-call(s32[1]{0:T(128)} %bitcast.me_ref, bf16[32,224,128]{2,1,0:T(8,128)(2,1)S(1)} %all_to_all.10.y_ref, bf16[32,32,128]{2,1,0:T(8,128)(2,1)S(1)} %collective-permute-done.other_ref, bf16[2,512,256]{2,1,0:T(8,128)(2,1)S(1)} %copy-done, bf16[2,256,512]{2,1,0:T(8,128)(2,1)S(1)} %copy-done.1), custom_call_target="tpu_custom_call" | custom-call | flops 5368709120 | bytes 5242880 | tf_op jit(solution)/shard_map/conv_attention/pallas_call | solution.py:221
  63.3 28.6 %all_to_all.11 = bf16[32,64,128]{2,1,0:T(8,128)(2,1)S(1)} all-to-all(bf16[32,64,128]{2,1,0:T(8,128)(2,1)S(1)} %conv_attention.1), channel_id=1, replica_groups=mesh['context'=32,'dp'=16] {'context'}, dimensions={0} | all-to-all | bytes 1048576 | tf_op jit(solution)/shard_map/all_to_all | solution.py:237
  91.8 0.9 copy_bitcast_fusion
  (1 shorter events, 0.0 us)
Async XLA Ops:
  2.3 56.2 %copy-start = (bf16[2,512,256]{2,1,0:T(8,128)(2,1)S(1)}, bf16[2,512,256]{2,1,0:T(8,128)(2,1)}, u32[]{:S(2)}) copy-start(bf16[2,512,256]{2,1,0:T(8,128)(2,1)} %constant.10.clone.fwd_ref) | copy-start | bytes 1572868
  2.3 56.1 %copy-start.1 = (bf16[2,256,512]{2,1,0:T(8,128)(2,1)S(1)}, bf16[2,256,512]{2,1,0:T(8,128)(2,1)}, u32[]{:S(2)}) copy-start(bf16[2,256,512]{2,1,0:T(8,128)(2,1)} %constant.11.clone.inv_ref) | copy-start | bytes 1572868
  55.0 3.5 %collective-permute-start = (bf16[32,32,128]{2,1,0:T(8,128)(2,1)S(1)}, bf16[32,32,128]{2,1,0:T(8,128)(2,1)S(1)}, u32[]{:S(2)}, u32[]{:S(2)}) collective-permute-start(bf16[32,32,128]{2,1,0:T(8,128)(2,1)S(1)} %slice.4), channel_id=1, source_target_pairs={{0,16},{16,0},{32,48},{48,32},{64,80},{80,64},{96,112},{112,96},{1... | collective-permute-start | bytes 786440 | tf_op jit(solution)/shard_map/ppermute | solution.py:219

commit v3 on v2

--- a/solution.py
+++ b/solution.py
@@ -103,8 +103,27 @@
     )(hyena_in, keys, values, filt)
 
 
+def spectra_kernel(y_ref, fwd_ref, spec):
+    sources, _, width = y_ref.shape
+    tok = BLOCK // 4
+    half = tok // 2
+    per = BLOCK // tok
+    blocks = sources // per
+    for pair in range(blocks // 2):
+        x_both = jnp.concatenate(
+            [
+                y_ref[block * per : (block + 1) * per, :tok, :].reshape(BLOCK, width)
+                for block in (2 * pair, 2 * pair + 1)
+            ],
+            axis=1,
+        )
+        got = dot(fwd_ref[...], jnp.concatenate([x_both, x_both], axis=0))
+        spec[2 * pair] = got[:, :width]
+        spec[2 * pair + 1] = got[:, width:]
+
+
 def main_kernel(
-    me_ref, y_ref, other_ref, fwd_ref, inv_ref, out_ref, spec, fspec, filt, bias, queries
+    me_ref, y_ref, other_ref, spec, fwd_ref, inv_ref, out_ref, total, fspec, filt, bias, queries
 ):
     sources, _, width = y_ref.shape
     tok = out_ref.shape[1]
@@ -119,24 +138,16 @@
         filt[pl.ds(at, half), :] = other_ref[source]
 
     for pair in range(blocks // 2):
-        x_both = jnp.concatenate(
-            [
-                y_ref[block * per : (block + 1) * per, :tok, :].reshape(BLOCK, width)
-                for block in (2 * pair, 2 * pair + 1)
-            ],
-            axis=1,
-        )
-        f_both = jnp.concatenate(
+        both = jnp.concatenate(
             [
                 filt[block * BLOCK : (block + 1) * BLOCK, :]
                 for block in (2 * pair, 2 * pair + 1)
             ],
             axis=1,
         )
-        for both, result in ((x_both, spec), (f_both, fspec)):
-            got = dot(fwd_ref[0], both) + dot(fwd_ref[1], both)
-            result[2 * pair] = got[:, :width]
-            result[2 * pair + 1] = got[:, width:]
+        got = dot(fwd_ref[...], jnp.concatenate([both, both], axis=0))
+        fspec[2 * pair] = got[:, :width]
+        fspec[2 * pair + 1] = got[:, width:]
 
     sign = 1.0 - 2.0 * (lax.broadcasted_iota(jnp.int32, (8, width), 0) % 2).astype(jnp.float32)
 
@@ -164,13 +175,13 @@
                 p = p_new if p is None else p + p_new
                 q = q_new if q is None else q + q_new
                 r = r_new if r is None else r + r_new
-            spec[block, low, :] = p - q
-            spec[block, high, :] = r - (p + q)
+            total[block, low, :] = p - q
+            total[block, high, :] = r - (p + q)
         return carry
 
-    lax.fori_loop(0, BLOCK // 8, products, 0, unroll=4)
+    lax.fori_loop(0, BLOCK // 8, products, 0, unroll=BLOCK // 8)
     for pair in range(blocks // 2):
-        value = jnp.concatenate([spec[2 * pair], spec[2 * pair + 1]], axis=1)
+        value = jnp.concatenate([total[2 * pair], total[2 * pair + 1]], axis=1)
         hi = value.astype(jnp.bfloat16)
         lo = (value - hi.astype(jnp.float32)).astype(jnp.bfloat16)
         conv = dot(inv_ref[0], hi) + (dot(inv_ref[0], lo) + dot(inv_ref[1], hi))
@@ -180,8 +191,8 @@
 
     reach = TILE // tok
     factor = math.log2(math.e) / math.sqrt(HEAD_DIM)
-    row = lax.broadcasted_iota(jnp.int32, (TILE, 2 * TILE), 0)
-    col = lax.broadcasted_iota(jnp.int32, (TILE, 2 * TILE), 1)
+    row = lax.broadcasted_iota(jnp.int32, (2 * TILE, TILE), 1)
+    col = lax.broadcasted_iota(jnp.int32, (2 * TILE, TILE), 0)
     allowed = (col <= row + TILE) & (col >= row // tok * tok)
     bias[...] = jnp.where(allowed, 0.0, -1e30)
     for tile in range(sources // reach):
@@ -192,14 +203,16 @@
         val = y_ref[first:last, 2 * tok : 3 * tok, :].reshape(span, width)
         query = queries[tile * TILE : (tile + 1) * TILE, :]
         scores = lax.dot_general(
-            query, key, (((1,), (1,)), ((), ())), preferred_element_type=jnp.float32
-        )
-        scores = scores + bias[:, 2 * TILE - span :]
-        top = jnp.max(scores, axis=-1, keepdims=True)
+            key, query, (((1,), (1,)), ((), ())), preferred_element_type=jnp.float32
+        )
+        scores = scores + bias[2 * TILE - span :, :]
+        top = jnp.max(scores, axis=0, keepdims=True)
         expo = jnp.exp2((scores - top) * factor)
-        probs = (expo * (1.0 / jnp.sum(expo, axis=-1, keepdims=True))).astype(jnp.bfloat16)
-        mixed = dot(probs, val).astype(jnp.bfloat16)
-        out_ref[tile * reach : last] = mixed.reshape(reach, tok, width)
+        probs = (expo * (1.0 / jnp.sum(expo, axis=0, keepdims=True))).astype(jnp.bfloat16)
+        mixed = lax.dot_general(
+            probs, val, (((0,), (0,)), ((), ())), preferred_element_type=jnp.float32
+        )
+        out_ref[tile * reach : last] = mixed.astype(jnp.bfloat16).reshape(reach, tok, width)
 
 
 def vmem(count):
@@ -210,7 +223,8 @@
     peers = lax.axis_size("context")
     tok, width = hyena_in.shape
     blocks = peers * tok // BLOCK
-    fwd = jnp.asarray(bf16_parts(forward_table(), 2))
+    hi, lo = bf16_parts(forward_table(), 2)
+    fwd = jnp.asarray(np.concatenate([hi, lo], axis=1))
     inv = jnp.asarray(bf16_parts(inverse_table(), 2))
     me = lax.axis_index("context").astype(jnp.int32).reshape(1)
 
@@ -218,22 +232,31 @@
     moved = lax.all_to_all(packed, "context", split_axis=0, concat_axis=0, tiled=True)
     other = lax.ppermute(moved[:, 3 * tok :], "context", [(i, i ^ 1) for i in range(peers)])
 
+    spectra = pl.pallas_call(
+        spectra_kernel,
+        out_shape=jax.ShapeDtypeStruct((blocks, 2 * BLOCK, HEAD_DIM), jnp.float32),
+        in_specs=vmem(2),
+        out_specs=vmem(1)[0],
+        compiler_params=pltpu.CompilerParams(vmem_limit_bytes=VMEM_LIMIT),
+        cost_estimate=pl.CostEstimate(flops=1 << 29, bytes_accessed=1 << 20, transcendentals=0),
+        name="spectra",
+    )(moved, fwd)
     mixed = pl.pallas_call(
         main_kernel,
         out_shape=jax.ShapeDtypeStruct((peers, tok, HEAD_DIM), jnp.bfloat16),
-        in_specs=[pl.BlockSpec(memory_space=pltpu.SMEM)] + vmem(4),
+        in_specs=[pl.BlockSpec(memory_space=pltpu.SMEM)] + vmem(5),
         out_specs=vmem(1)[0],
         scratch_shapes=[
             pltpu.VMEM((blocks, 2 * BLOCK, HEAD_DIM), jnp.float32),
             pltpu.VMEM((blocks, 2 * BLOCK, HEAD_DIM), jnp.float32),
             pltpu.VMEM((peers * tok, HEAD_DIM), jnp.bfloat16),
-            pltpu.VMEM((TILE, 2 * TILE), jnp.float32),
+            pltpu.VMEM((2 * TILE, TILE), jnp.float32),
             pltpu.VMEM((peers * tok, HEAD_DIM), jnp.bfloat16),
         ],
         compiler_params=pltpu.CompilerParams(vmem_limit_bytes=VMEM_LIMIT),
         cost_estimate=pl.CostEstimate(flops=5 << 30, bytes_accessed=5 << 20, transcendentals=1 << 19),
         name="conv_attention",
-    )(me, moved, other, fwd, inv)
+    )(me, moved, other, spectra, fwd, inv)
     home = lax.all_to_all(mixed, "context", split_axis=0, concat_axis=0, tiled=True)
     return home.transpose(1, 0, 2).reshape(tok, width)
 

time: 93.5 us -> 92.3 us (0.987)
    pallas_call x1, Pallas kernels: 4.82 us -> 3.66 us  [local(): pl.pallas_call(main_kernel, out_shape=jax.ShapeDtypeStruct((peers, tok, H...]
  transfers between devices with their start and end apart: 1 -> 1, of which waited for: 1 -> 1; matrix products, arithmetic and copies ran while one was open for 0% -> 0% of each run, Pallas kernels for 0% -> 1%
where the time goes in v3:
time: 92.3 us; the launch traced here: 91.5 us
  blocking collectives  81.2 us (88%)
  Pallas kernels  6.66 us (7%)
  starting transfers between devices  2.31 us (3%)
    all_to_all x1, blocking collectives, local(): lax.all_to_all(packed, 'context', split_axis=0, concat_axis=0, tiled=True)  52.6 us
    all_to_all x1, blocking collectives, local(): lax.all_to_all(mixed, 'context', split_axis=0, concat_axis=0, tiled=True)  28.6 us
    pallas_call x1, Pallas kernels, local(): pl.pallas_call(main_kernel, out_shape=jax.ShapeDtypeStruct((peers, tok, H...  3.66 us
    ppermute x1, starting transfers between devices, local(): lax.ppermute(moved[:, 3 * tok:], 'context', [(i, i ^ 1) for i in range(pe...  2.31 us
    pallas_call x1, Pallas kernels, pack(): pl.pallas_call(pack_kernel, out_shape=jax.ShapeDtypeStruct(shape, jnp.bfl...  2.28 us
  transfers between devices with their start and end apart: 1, of which 1 were waited for; matrix products, arithmetic and copies ran while one was open for 0% of the time, Pallas kernels for 1%

profile of v3, /device:TPU:1, one launch (start us, length us, event | category | flops | bytes accessed | tf_op | source)
XLA Modules:
  0.0 91.5 jit_solution(5580728670108459198)
XLA Ops:
  0.0 2.3 %pack.1 = bf16[32,224,128]{2,1,0:T(8,128)(2,1)} custom-call(bf16[64,4096]{1,0:T(8,128)(2,1)} %x_ref.1, bf16[64,4096]{1,0:T(8,128)(2,1)} %k_ref.1, bf16[64,4096]{1,0:T(8,128)(2,1)} %v_ref.1, bf16[64,128]{1,0:T(8,128)(2,1)} %f_ref.1), custom_call_target="tpu_custom_call" | custom-call | bytes 3670016 | tf_op jit(solution)/shard_map/pack/pallas_call | solution.py:88
  2.3 0.0 copy-start
  2.3 52.6 %all_to_all.10.y_ref = bf16[32,224,128]{2,1,0:T(8,128)(2,1)S(1)} all-to-all(bf16[32,224,128]{2,1,0:T(8,128)(2,1)} %pack.1), channel_id=1, replica_groups=mesh['context'=32,'dp'=16] {'context'}, dimensions={0} | all-to-all | bytes 3670016 | tf_op jit(solution)/shard_map/all_to_all | solution.py:232
  55.0 2.3 %collective-permute-start = (bf16[32,32,128]{2,1,0:T(8,128)(2,1)S(1)}, bf16[32,32,128]{2,1,0:T(8,128)(2,1)S(1)}, u32[]{:S(2)}, u32[]{:S(2)}) collective-permute-start(bf16[32,32,128]{2,1,0:T(8,128)(2,1)S(1)} %slice.4), channel_id=1, source_target_pairs={{0,16},{16,0},{32,48},{48,32},{64,80},{80,64},{96,112},{112,96},{1... | collective-permute-start | bytes 786440 | tf_op jit(solution)/shard_map/ppermute | solution.py:233
  57.3 0.0 copy-done
  57.3 0.0 copy-start.1
  57.3 0.7 spectra.1.spec
  58.0 0.4 collective-permute-done.other_ref
  58.4 0.0 copy-done.1
  58.4 3.7 %conv_attention.1 = bf16[32,64,128]{2,1,0:T(8,128)(2,1)S(1)} custom-call(s32[1]{0:T(128)} %bitcast.me_ref, bf16[32,224,128]{2,1,0:T(8,128)(2,1)S(1)} %all_to_all.10.y_ref, bf16[32,32,128]{2,1,0:T(8,128)(2,1)S(1)} %collective-permute-done.other_ref, f32[8,512,128]{2,1,0:T(8,128)S(1)} %spectra.1.spec, bf16[512,512]{1,0:T(8,128)(2,1)S(1)} %copy-done, ...), custom_call_target="tpu_custom_call" | custom-call | flops 5368709120 | bytes 5242880 | tf_op jit(solution)/shard_map/conv_attention/pallas_call | solution.py:244
  62.1 28.6 %all_to_all.11 = bf16[32,64,128]{2,1,0:T(8,128)(2,1)S(1)} all-to-all(bf16[32,64,128]{2,1,0:T(8,128)(2,1)S(1)} %conv_attention.1), channel_id=1, replica_groups=mesh['context'=32,'dp'=16] {'context'}, dimensions={0} | all-to-all | bytes 1048576 | tf_op jit(solution)/shard_map/all_to_all | solution.py:260
  90.7 0.9 copy_bitcast_fusion
  (1 shorter events, 0.0 us)
Async XLA Ops:
  2.3 55.0 %copy-start = (bf16[512,512]{1,0:T(8,128)(2,1)S(1)}, bf16[512,512]{1,0:T(8,128)(2,1)}, u32[]{:S(2)}) copy-start(bf16[512,512]{1,0:T(8,128)(2,1)} %constant.10.clone.fwd_ref) | copy-start | bytes 1572868
  55.0 3.5 %collective-permute-start = (bf16[32,32,128]{2,1,0:T(8,128)(2,1)S(1)}, bf16[32,32,128]{2,1,0:T(8,128)(2,1)S(1)}, u32[]{:S(2)}, u32[]{:S(2)}) collective-permute-start(bf16[32,32,128]{2,1,0:T(8,128)(2,1)S(1)} %slice.4), channel_id=1, source_target_pairs={{0,16},{16,0},{32,48},{48,32},{64,80},{80,64},{96,112},{112,96},{1... | collective-permute-start | bytes 786440 | tf_op jit(solution)/shard_map/ppermute | solution.py:233
  57.3 1.1 %copy-start.1 = (bf16[2,256,512]{2,1,0:T(8,128)(2,1)S(1)}, bf16[2,256,512]{2,1,0:T(8,128)(2,1)}, u32[]{:S(2)}) copy-start(bf16[2,256,512]{2,1,0:T(8,128)(2,1)} %constant.11.clone.inv_ref) | copy-start | bytes 1572868

commit v4 on v2

--- a/solution.py
+++ b/solution.py
@@ -14,6 +14,8 @@
 TILE = 128
 VMEM_LIMIT = 48 * 1024 * 1024
 CHUNKS = 4
+CONV_COST = 1024
+RECURSE = False
 
 
 def bf16_parts(table, count):
@@ -48,26 +50,37 @@
     return pltpu.make_async_copy(src, dst, sem)
 
 
-def pack_kernel(x_ref, k_ref, v_ref, f_ref, out_ref, held, half, load, store):
+def pack_kernel(
+    me_ref, x_ref, k_ref, v_ref, f_ref, out_ref, near_ref, far_ref, held, kept, half, load, store
+):
     tok, width = x_ref.shape
     heads = width // HEAD_DIM
     group = heads // CHUNKS
     part = tok // 2
+    me = me_ref[0]
     filters = copy(f_ref, half, load.at[CHUNKS])
     filters.start()
     loads = [[] for _ in range(CHUNKS)]
+    loads_v = []
     for head in range(heads):
         cols = pl.ds(head * HEAD_DIM, HEAD_DIM)
-        for place, ref in enumerate((x_ref, k_ref, v_ref)):
+        for place, ref in enumerate((x_ref, k_ref)):
             step = copy(
                 ref.at[:, cols], held.at[head, pl.ds(place * tok, tok)], load.at[head // group]
             )
             step.start()
             loads[head // group].append(step)
+    for head in range(heads):
+        cols = pl.ds(head * HEAD_DIM, HEAD_DIM)
+        apart = lax.bitwise_xor(me, jnp.int32(head))
+        place = lax.bitwise_and(apart, 1) * (heads // 2) + lax.shift_right_logical(apart, 1)
+        step = copy(v_ref.at[:, cols], kept.at[place], load.at[CHUNKS + 1])
+        step.start()
+        loads_v.append(step)
     filters.wait()
     for head in range(heads):
         first = head % 2 * part
-        held[head, 3 * tok :, :] = half[first : first + part, :]
+        held[head, 2 * tok :, :] = half[first : first + part, :]
     stores = []
     for chunk in range(CHUNKS):
         for step in loads[chunk]:
@@ -76,47 +89,72 @@
         step = copy(held.at[some], out_ref.at[some], store.at[chunk])
         step.start()
         stores.append(step)
+    for step in loads_v:
+        step.wait()
+    for number, ref in enumerate((near_ref, far_ref)):
+        step = copy(
+            kept.at[pl.ds(number * (heads // 2), heads // 2)], ref, store.at[CHUNKS + number]
+        )
+        step.start()
+        stores.append(step)
     for step in stores:
         step.wait()
 
 
-def pack(hyena_in, keys, values, filt):
+def pack(me, hyena_in, keys, values, filt):
     tok, width = hyena_in.shape
     heads = width // HEAD_DIM
-    shape = (heads, 3 * tok + tok // 2, HEAD_DIM)
+    shape = (heads, 2 * tok + tok // 2, HEAD_DIM)
+    shape_v = (heads // 2, tok, HEAD_DIM)
     anywhere = pl.BlockSpec(memory_space=pl.ANY)
     return pl.pallas_call(
         pack_kernel,
-        out_shape=jax.ShapeDtypeStruct(shape, jnp.bfloat16),
-        in_specs=[anywhere] * 4,
-        out_specs=anywhere,
+        out_shape=[jax.ShapeDtypeStruct(some, jnp.bfloat16) for some in (shape, shape_v, shape_v)],
+        in_specs=[pl.BlockSpec(memory_space=pltpu.SMEM)] + [anywhere] * 4,
+        out_specs=[anywhere] * 3,
         scratch_shapes=[
             pltpu.VMEM(shape, jnp.bfloat16),
+            pltpu.VMEM((heads, tok, HEAD_DIM), jnp.bfloat16),
             pltpu.VMEM((tok, HEAD_DIM), jnp.bfloat16),
-            pltpu.SemaphoreType.DMA((CHUNKS + 1,)),
-            pltpu.SemaphoreType.DMA((CHUNKS,)),
+            pltpu.SemaphoreType.DMA((CHUNKS + 2,)),
+            pltpu.SemaphoreType.DMA((CHUNKS + 2,)),
         ],
         cost_estimate=pl.CostEstimate(
             flops=0, bytes_accessed=14 * tok * width, transcendentals=0
         ),
         name="pack",
-    )(hyena_in, keys, values, filt)
-
-
-def main_kernel(
-    me_ref, y_ref, other_ref, fwd_ref, inv_ref, out_ref, spec, fspec, filt, bias, queries
+    )(me, hyena_in, keys, values, filt)
+
+
+def conv_kernel(
+    me_ref,
+    y_ref,
+    other_ref,
+    fwd_ref,
+    inv_ref,
+    out_ref,
+    spec,
+    fspec,
+    filt,
+    bias,
+    queries,
 ):
     sources, _, width = y_ref.shape
-    tok = out_ref.shape[1]
-    half = tok // 2
+    half = other_ref.shape[1]
+    tok = 2 * half
     per = BLOCK // tok
     blocks = sources // per
     odd = lax.bitwise_and(me_ref[0], 1)
     for source in range(sources):
-        at = pl.multiple_of(source * tok + odd * half, half)
-        filt[pl.ds(at, half), :] = y_ref[source, 3 * tok : 3 * tok + half, :]
         at = pl.multiple_of(source * tok + (1 - odd) * half, half)
         filt[pl.ds(at, half), :] = other_ref[source]
+    row = lax.broadcasted_iota(jnp.int32, (2 * TILE, TILE), 1)
+    col = lax.broadcasted_iota(jnp.int32, (2 * TILE, TILE), 0)
+    allowed = (col <= row + TILE) & (col >= row // tok * tok)
+    bias[...] = jnp.where(allowed, 0.0, -1e30)
+    for source in range(sources):
+        at = pl.multiple_of(source * tok + odd * half, half)
+        filt[pl.ds(at, half), :] = y_ref[source, 2 * tok :, :]
 
     for pair in range(blocks // 2):
         x_both = jnp.concatenate(
@@ -134,7 +172,7 @@
             axis=1,
         )
         for both, result in ((x_both, spec), (f_both, fspec)):
-            got = dot(fwd_ref[0], both) + dot(fwd_ref[1], both)
+            got = dot(fwd_ref[...], jnp.concatenate([both, both], axis=0))
             result[2 * pair] = got[:, :width]
             result[2 * pair + 1] = got[:, width:]
 
@@ -168,7 +206,7 @@
             spec[block, high, :] = r - (p + q)
         return carry
 
-    lax.fori_loop(0, BLOCK // 8, products, 0, unroll=4)
+    lax.fori_loop(0, BLOCK // 8, products, 0, unroll=BLOCK // 8)
     for pair in range(blocks // 2):
         value = jnp.concatenate([spec[2 * pair], spec[2 * pair + 1]], axis=1)
         hi = value.astype(jnp.bfloat16)
@@ -180,60 +218,121 @@
 
     reach = TILE // tok
     factor = math.log2(math.e) / math.sqrt(HEAD_DIM)
-    row = lax.broadcasted_iota(jnp.int32, (TILE, 2 * TILE), 0)
-    col = lax.broadcasted_iota(jnp.int32, (TILE, 2 * TILE), 1)
-    allowed = (col <= row + TILE) & (col >= row // tok * tok)
-    bias[...] = jnp.where(allowed, 0.0, -1e30)
     for tile in range(sources // reach):
         first = max(tile * reach - reach, 0)
         last = (tile + 1) * reach
         span = (last - first) * tok
         key = y_ref[first:last, tok : 2 * tok, :].reshape(span, width)
-        val = y_ref[first:last, 2 * tok : 3 * tok, :].reshape(span, width)
         query = queries[tile * TILE : (tile + 1) * TILE, :]
         scores = lax.dot_general(
-            query, key, (((1,), (1,)), ((), ())), preferred_element_type=jnp.float32
-        )
-        scores = scores + bias[:, 2 * TILE - span :]
-        top = jnp.max(scores, axis=-1, keepdims=True)
+            key, query, (((1,), (1,)), ((), ())), preferred_element_type=jnp.float32
+        )
+        scores = scores + bias[2 * TILE - span :, :]
+        top = jnp.max(scores, axis=0, keepdims=True)
         expo = jnp.exp2((scores - top) * factor)
-        probs = (expo * (1.0 / jnp.sum(expo, axis=-1, keepdims=True))).astype(jnp.bfloat16)
-        mixed = dot(probs, val).astype(jnp.bfloat16)
-        out_ref[tile * reach : last] = mixed.reshape(reach, tok, width)
+        probs = expo * (1.0 / jnp.sum(expo, axis=0, keepdims=True))
+        out_ref[tile, 2 * TILE - span :, :] = probs.astype(jnp.bfloat16)
+
+
+def mix_kernel(me_ref, probs_ref, *refs):
+    pieces, out_ref, val = refs[:-2], refs[-2], refs[-1]
+    sources, tok, width = val.shape
+    me = me_ref[0]
+    for along_z, ref in enumerate(pieces):
+        for core in range(2):
+            for along_x in range(ref.shape[1]):
+                apart = along_x * 8 + along_z * 2 + core
+                val[lax.bitwise_xor(me, jnp.int32(apart))] = ref[core, along_x]
+    reach = TILE // tok
+    for tile in range(sources // reach):
+        first = max(tile * reach - reach, 0)
+        last = (tile + 1) * reach
+        span = (last - first) * tok
+        mixed = lax.dot_general(
+            probs_ref[tile, 2 * TILE - span :, :],
+            val[first:last].reshape(span, width),
+            (((0,), (0,)), ((), ())),
+            preferred_element_type=jnp.float32,
+        )
+        out_ref[tile * reach : last] = mixed.astype(jnp.bfloat16).reshape(reach, tok, width)
 
 
 def vmem(count):
     return [pl.BlockSpec(memory_space=pltpu.VMEM)] * count
+
+
+def swap(array, bits):
+    peers = lax.axis_size("context")
+    return lax.ppermute(array, "context", [(i, i ^ bits) for i in range(peers)])
+
+
+def route(near, far):
+    _, tok, width = near.shape
+    near = near.reshape(4, 4, tok, width)
+    other = swap(far, 1).reshape(4, 4, tok, width)
+    if RECURSE:
+        both = jnp.stack([near, other])
+        step = swap(jnp.stack([both[:, 1], both[:, 3]]), 8)
+        last = swap(jnp.stack([both[:, 2], step[1]]), 16)
+        arrived = [both[:, 0], step[0], last[0], last[1]]
+    else:
+        arrived = []
+        for along_x in range(4):
+            both = jnp.stack([near[along_x], other[along_x]])
+            arrived.append(swap(both, along_x * 8) if along_x else both)
+    pieces = []
+    for along_z in range(4):
+        mine = jnp.stack([some[:, along_z] for some in arrived], axis=1)
+        pieces.append(swap(mine, along_z * 2) if along_z else mine)
+    return pieces
 
 
 def local(hyena_in, filt, keys, values):
     peers = lax.axis_size("context")
     tok, width = hyena_in.shape
     blocks = peers * tok // BLOCK
-    fwd = jnp.asarray(bf16_parts(forward_table(), 2))
+    tiles = peers * tok // TILE
+    hi, lo = bf16_parts(forward_table(), 2)
+    fwd = jnp.asarray(np.concatenate([hi, lo], axis=1))
     inv = jnp.asarray(bf16_parts(inverse_table(), 2))
     me = lax.axis_index("context").astype(jnp.int32).reshape(1)
-
-    packed = pack(hyena_in, keys, values, filt)
+    params = pltpu.CompilerParams(vmem_limit_bytes=VMEM_LIMIT)
+    scalar = pl.BlockSpec(memory_space=pltpu.SMEM)
+
+    packed, near, far = pack(me, hyena_in, keys, values, filt)
     moved = lax.all_to_all(packed, "context", split_axis=0, concat_axis=0, tiled=True)
-    other = lax.ppermute(moved[:, 3 * tok :], "context", [(i, i ^ 1) for i in range(peers)])
-
-    mixed = pl.pallas_call(
-        main_kernel,
-        out_shape=jax.ShapeDtypeStruct((peers, tok, HEAD_DIM), jnp.bfloat16),
-        in_specs=[pl.BlockSpec(memory_space=pltpu.SMEM)] + vmem(4),
+    pieces = route(near, far)
+    mine = moved[:, 2 * tok :]
+    pairs = [[i, i + 1] for i in range(0, peers, 2)]
+    both = lax.all_to_all(jnp.stack([mine, mine]), "context", 0, 0, axis_index_groups=pairs, tiled=True)
+    other = jnp.where(me[0] % 2 == 1, both[0], both[1])
+
+    probs = pl.pallas_call(
+        conv_kernel,
+        out_shape=jax.ShapeDtypeStruct((tiles, 2 * TILE, TILE), jnp.bfloat16),
+        in_specs=[scalar] + vmem(4),
         out_specs=vmem(1)[0],
         scratch_shapes=[
             pltpu.VMEM((blocks, 2 * BLOCK, HEAD_DIM), jnp.float32),
             pltpu.VMEM((blocks, 2 * BLOCK, HEAD_DIM), jnp.float32),
             pltpu.VMEM((peers * tok, HEAD_DIM), jnp.bfloat16),
-            pltpu.VMEM((TILE, 2 * TILE), jnp.float32),
+            pltpu.VMEM((2 * TILE, TILE), jnp.float32),
             pltpu.VMEM((peers * tok, HEAD_DIM), jnp.bfloat16),
         ],
-        compiler_params=pltpu.CompilerParams(vmem_limit_bytes=VMEM_LIMIT),
+        compiler_params=params,
         cost_estimate=pl.CostEstimate(flops=5 << 30, bytes_accessed=5 << 20, transcendentals=1 << 19),
-        name="conv_attention",
+        name="conv_probs",
     )(me, moved, other, fwd, inv)
+    mixed = pl.pallas_call(
+        mix_kernel,
+        out_shape=jax.ShapeDtypeStruct((peers, tok, HEAD_DIM), jnp.bfloat16),
+        in_specs=[scalar] + vmem(5),
+        out_specs=vmem(1)[0],
+        scratch_shapes=[pltpu.VMEM((peers, tok, HEAD_DIM), jnp.bfloat16)],
+        compiler_params=params,
+        cost_estimate=pl.CostEstimate(flops=1 << 28, bytes_accessed=2 << 20, transcendentals=0),
+        name="mix",
+    )(me, probs, *pieces)
     home = lax.all_to_all(mixed, "context", split_axis=0, concat_axis=0, tiled=True)
     return home.transpose(1, 0, 2).reshape(tok, width)
 

time: 93.5 us -> 89.1 us (0.953)
  blocking collectives: 81.2 us -> 30.2 us
  starting transfers between devices: 2.31 us -> 37.7 us
  waiting for transfers between devices: 1.14 us -> 12.6 us
    all_to_all x1, blocking collectives: 52.6 us -> 5.54 us  [local(): lax.all_to_all(jnp.stack([mine, mine]), 'context', 0, 0, axis_index_group...]
    ppermute x1 -> x7, starting transfers between devices: 2.31 us -> 23.2 us  [swap(): return lax.ppermute(array, 'context', [(i, i ^ bits) for i in range(peers)])]
    all_to_all x0 -> x1, starting transfers between devices: none -> 14.6 us  [local(): lax.all_to_all(packed, 'context', split_axis=0, concat_axis=0, tiled=True)]
    ppermute x1 -> x7, waiting for transfers between devices: 1.14 us -> 12.6 us  [swap(): return lax.ppermute(array, 'context', [(i, i ^ bits) for i in range(peers)])]
    all_to_all x1, blocking collectives: 28.6 us -> 24.6 us  [local(): lax.all_to_all(mixed, 'context', split_axis=0, concat_axis=0, tiled=True)]
    pallas_call x2 -> x3, Pallas kernels: 7.1 us -> 6.6 us  [the longest x1 3.81 us: local(): pl.pallas_call(conv_kernel, out_shape=jax.ShapeDtypeStruct((tiles, 2 * TI...]
  transfers between devices with their start and end apart: 1 -> 8, of which waited for: 1 -> 4; matrix products, arithmetic and copies ran while one was open for 0% -> 0% of each run, Pallas kernels for 0% -> 4%
where the time goes in v4:
time: 89.1 us; the launch traced here: 88.6 us
  starting transfers between devices  37.7 us (42%)
  blocking collectives  30.2 us (34%)
  waiting for transfers between devices  12.6 us (14%)
  Pallas kernels  6.6 us (7%)
  local copies, waits for them, and re-layouts  0.97 us (1%)
    all_to_all x1, blocking collectives, local(): lax.all_to_all(mixed, 'context', split_axis=0, concat_axis=0, tiled=True)  24.6 us
    ppermute x7, starting transfers between devices, swap(): return lax.ppermute(array, 'context', [(i, i ^ bits) for i in range(peers)])  23.2 us
    all_to_all x1, starting transfers between devices, local(): lax.all_to_all(packed, 'context', split_axis=0, concat_axis=0, tiled=True)  14.6 us
    ppermute x7, waiting for transfers between devices, swap(): return lax.ppermute(array, 'context', [(i, i ^ bits) for i in range(peers)])  12.6 us
    all_to_all x1, blocking collectives, local(): lax.all_to_all(jnp.stack([mine, mine]), 'context', 0, 0, axis_index_group...  5.54 us
    pallas_call x1, Pallas kernels, local(): pl.pallas_call(conv_kernel, out_shape=jax.ShapeDtypeStruct((tiles, 2 * TI...  3.81 us
    pallas_call x1, Pallas kernels, pack(): pl.pallas_call(pack_kernel, out_shape=[jax.ShapeDtypeStruct(some, jnp.bfl...  2.3 us
  transfers between devices with their start and end apart: 8, of which 4 were waited for; matrix products, arithmetic and copies ran while one was open for 0% of the time, Pallas kernels for 4%

profile of v4, /device:TPU:1, one launch (start us, length us, event | category | flops | bytes accessed | tf_op | source)
XLA Modules:
  0.0 88.6 jit_solution(13755184366045725272)
XLA Ops:
  0.0 2.3 %pack.1 = (bf16[32,160,128]{2,1,0:T(8,128)(2,1)}, bf16[16,64,128]{2,1,0:T(8,128)(2,1)}, bf16[16,64,128]{2,1,0:T(8,128)(2,1)}) custom-call(s32[1]{0:T(128)} %bitcast.me_ref, bf16[64,4096]{1,0:T(8,128)(2,1)} %x_ref.1, bf16[64,4096]{1,0:T(8,128)(2,1)} %k_ref.1, bf16[64,4096]{1,0:T(8,128)(2,1)} %v_ref.1, bf16[64,128]{1,0:T(8,128)(2,1)} %f_ref.1), custom_call_target="tpu_custom_call" | custom-call | bytes 3670016 | tf_op jit(solution)/shard_map/pack/pallas_call | solution.py:110
  2.3 0.0 copy-start.3
  2.3 0.0 copy-start.2
  2.3 14.6 %all-to-all-start = ((bf16[32,160,128]{2,1,0:T(8,128)(2,1)}), bf16[32,160,128]{2,1,0:T(8,128)(2,1)S(1)}, u32[]{:S(2)}, u32[]{:S(2)}) async-start(bf16[32,160,128]{2,1,0:T(8,128)(2,1)} %get-tuple-element.8), calls=%async_computation | async-start | bytes 2621440 | tf_op jit(solution)/shard_map/all_to_all | solution.py:303
  16.9 0.0 copy-done.3
  16.9 2.1 %collective-permute-start = (bf16[16,64,128]{2,1,0:T(8,128)(2,1)S(1)}, bf16[16,64,128]{2,1,0:T(8,128)(2,1)S(1)}, u32[]{:S(2)}, u32[]{:S(2)}) collective-permute-start(bf16[16,64,128]{2,1,0:T(8,128)(2,1)S(1)} %copy-done.3), channel_id=1, source_target_pairs={{0,16},{16,0},{32,48},{48,32},{64,80},{80,64},{96,112},{112,96},{1... | collective-permute-start | bytes 786440 | tf_op jit(solution)/shard_map/ppermute | solution.py:266
  19.1 0.0 copy-done.2
  19.1 1.2 %collective-permute-done = bf16[16,64,128]{2,1,0:T(8,128)(2,1)S(1)} collective-permute-done((bf16[16,64,128]{2,1,0:T(8,128)(2,1)S(1)}, bf16[16,64,128]{2,1,0:T(8,128)(2,1)S(1)}, u32[]{:S(2)}, u32[]{:S(2)}) %collective-permute-start) | collective-permute-done | bytes 262176 | tf_op jit(solution)/shard_map/ppermute | solution.py:266
  20.4 4.5 %collective-permute-start.3 = (bf16[2,4,64,128]{3,2,1,0:T(8,128)(2,1)S(1)}, bf16[2,4,64,128]{3,2,1,0:T(8,128)(2,1)S(1)}, u32[]{:S(2)}, u32[]{:S(2)}) collective-permute-start(bf16[2,4,64,128]{3,2,1,0:T(8,128)(2,1)S(1)} %pad_maximum_fusion.4), channel_id=1, source_target_pairs={{0,384},{16,400},{32,416},{48,432},{64,448},{80,464},{96,480},{112... | collective-permute-start | bytes 393224 | tf_op jit(solution)/shard_map/ppermute | solution.py:266
  25.0 2.4 %collective-permute-start.2 = (bf16[2,4,64,128]{3,2,1,0:T(8,128)(2,1)S(1)}, bf16[2,4,64,128]{3,2,1,0:T(8,128)(2,1)S(1)}, u32[]{:S(2)}, u32[]{:S(2)}) collective-permute-start(bf16[2,4,64,128]{3,2,1,0:T(8,128)(2,1)S(1)} %pad_maximum_fusion.3), channel_id=1, source_target_pairs={{0,256},{16,272},{32,288},{48,304},{64,320},{80,336},{96,352},{112... | collective-permute-start | bytes 393224 | tf_op jit(solution)/shard_map/ppermute | solution.py:266
  27.4 2.0 %collective-permute-start.1 = (bf16[2,4,64,128]{3,2,1,0:T(8,128)(2,1)S(1)}, bf16[2,4,64,128]{3,2,1,0:T(8,128)(2,1)S(1)}, u32[]{:S(2)}, u32[]{:S(2)}) collective-permute-start(bf16[2,4,64,128]{3,2,1,0:T(8,128)(2,1)S(1)} %pad_maximum_fusion.2), channel_id=1, source_target_pairs={{0,128},{16,144},{32,160},{48,176},{64,192},{80,208},{96,224},{112... | collective-permute-start | bytes 393224 | tf_op jit(solution)/shard_map/ppermute | solution.py:266
  29.5 8.5 %collective-permute-done.3 = bf16[2,4,64,128]{3,2,1,0:T(8,128)(2,1)S(1)} collective-permute-done((bf16[2,4,64,128]{3,2,1,0:T(8,128)(2,1)S(1)}, bf16[2,4,64,128]{3,2,1,0:T(8,128)(2,1)S(1)}, u32[]{:S(2)}, u32[]{:S(2)}) %collective-permute-start.3) | collective-permute-done | bytes 131104 | tf_op jit(solution)/shard_map/ppermute | solution.py:266
  38.0 0.0 collective-permute-done.2
  38.0 1.2 %collective-permute-done.1 = bf16[2,4,64,128]{3,2,1,0:T(8,128)(2,1)S(1)} collective-permute-done((bf16[2,4,64,128]{3,2,1,0:T(8,128)(2,1)S(1)}, bf16[2,4,64,128]{3,2,1,0:T(8,128)(2,1)S(1)}, u32[]{:S(2)}, u32[]{:S(2)}) %collective-permute-start.1) | collective-permute-done | bytes 131104 | tf_op jit(solution)/shard_map/ppermute | solution.py:266
  39.3 4.9 %collective-permute-start.4 = (bf16[2,4,64,128]{3,2,1,0:T(8,128)(2,1)S(1)}, bf16[2,4,64,128]{3,2,1,0:T(8,128)(2,1)S(1)}, u32[]{:S(2)}, u32[]{:S(2)}) collective-permute-start(bf16[2,4,64,128]{3,2,1,0:T(8,128)(2,1)S(1)} %pad_maximum_fusion.6), channel_id=1, source_target_pairs={{0,32},{16,48},{32,0},{48,16},{64,96},{80,112},{96,64},{112,80},{1... | collective-permute-start | bytes 393224 | tf_op jit(solution)/shard_map/ppermute | solution.py:266
  44.2 4.8 %collective-permute-start.5 = (bf16[2,4,64,128]{3,2,1,0:T(8,128)(2,1)S(1)}, bf16[2,4,64,128]{3,2,1,0:T(8,128)(2,1)S(1)}, u32[]{:S(2)}, u32[]{:S(2)}) collective-permute-start(bf16[2,4,64,128]{3,2,1,0:T(8,128)(2,1)S(1)} %pad_maximum_fusion.7), channel_id=1, source_target_pairs={{0,64},{16,80},{32,96},{48,112},{64,0},{80,16},{96,32},{112,48},{1... | collective-permute-start | bytes 393224 | tf_op jit(solution)/shard_map/ppermute | solution.py:266
  49.1 2.3 %collective-permute-start.6 = (bf16[2,4,64,128]{3,2,1,0:T(8,128)(2,1)S(1)}, bf16[2,4,64,128]{3,2,1,0:T(8,128)(2,1)S(1)}, u32[]{:S(2)}, u32[]{:S(2)}) collective-permute-start(bf16[2,4,64,128]{3,2,1,0:T(8,128)(2,1)S(1)} %fusion.3), channel_id=1, source_target_pairs={{0,96},{16,112},{32,64},{48,80},{64,32},{80,48},{96,0},{112,16},{1... | collective-permute-start | bytes 393224 | tf_op jit(solution)/shard_map/ppermute | solution.py:266
  51.4 0.0 all-to-all-done.y_ref
  51.5 0.0 copy-start
  51.5 0.0 copy-start.1
  51.5 5.5 %all_to_all.15 = bf16[2,32,32,128]{3,2,1,0:T(8,128)(2,1)S(1)} all-to-all(bf16[2,32,32,128]{3,2,1,0:T(8,128)(2,1)S(1)} %pad_maximum_fusion), channel_id=1, replica_groups={{0,16},{32,48},{64,80},{96,112},{128,144},{160,176},{192,208},{224,240}..., dimensions={0} | all-to-all | bytes 1048576 | tf_op jit(solution)/shard_map/all_to_all | solution.py:307
  57.1 0.0 copy-done
  57.1 0.0 copy-done.1
  57.1 3.8 %conv_probs.1.probs_ref = bf16[16,256,128]{2,1,0:T(8,128)(2,1)S(1)} custom-call(s32[1]{0:T(128)} %bitcast.me_ref, bf16[32,160,128]{2,1,0:T(8,128)(2,1)S(1)} %all-to-all-done.y_ref, bf16[32,32,128]{2,1,0:T(8,128)(2,1)S(1)} %fusion.other_ref, bf16[512,512]{1,0:T(8,128)(2,1)S(1)} %copy-done, bf16[2,256,512]{2,1,0:T(8,128)(2,1)S(1)} %copy-done.1), custom_call_target="tpu_custom_call" | custom-call | flops 5368709120 | bytes 5242880 | tf_op jit(solution)/shard_map/conv_probs/pallas_call | solution.py:310
  60.9 0.0 collective-permute-done.4.refs_1_
  61.0 1.6 %collective-permute-done.5.refs_2_ = bf16[2,4,64,128]{3,2,1,0:T(8,128)(2,1)S(1)} collective-permute-done((bf16[2,4,64,128]{3,2,1,0:T(8,128)(2,1)S(1)}, bf16[2,4,64,128]{3,2,1,0:T(8,128)(2,1)S(1)}, u32[]{:S(2)}, u32[]{:S(2)}) %collective-permute-start.5) | collective-permute-done | bytes 131104 | tf_op jit(solution)/shard_map/ppermute | solution.py:266
  62.6 0.0 collective-permute-done.6.refs_3_
  62.6 0.5 mix.1
  63.1 24.6 %all_to_all.16 = bf16[32,64,128]{2,1,0:T(8,128)(2,1)S(1)} all-to-all(bf16[32,64,128]{2,1,0:T(8,128)(2,1)S(1)} %mix.1), channel_id=1, replica_groups=mesh['context'=32,'dp'=16] {'context'}, dimensions={0} | all-to-all | bytes 1048576 | tf_op jit(solution)/shard_map/all_to_all | solution.py:336
  87.7 0.9 copy_bitcast_fusion
  (16 shorter events, 0.3 us)
Async XLA Ops:
  2.3 14.6 %copy-start.3 = (bf16[16,64,128]{2,1,0:T(8,128)(2,1)S(1)}, bf16[16,64,128]{2,1,0:T(8,128)(2,1)}, u32[]{:S(2)}) copy-start(bf16[16,64,128]{2,1,0:T(8,128)(2,1)} %get-tuple-element.10) | copy-start | bytes 786436
  2.3 16.8 %copy-start.2 = (bf16[16,64,128]{2,1,0:T(8,128)(2,1)S(1)}, bf16[16,64,128]{2,1,0:T(8,128)(2,1)}, u32[]{:S(2)}) copy-start(bf16[16,64,128]{2,1,0:T(8,128)(2,1)} %get-tuple-element.9) | copy-start | bytes 786436
  2.3 49.1 %all-to-all-start = ((bf16[32,160,128]{2,1,0:T(8,128)(2,1)}), bf16[32,160,128]{2,1,0:T(8,128)(2,1)S(1)}, u32[]{:S(2)}, u32[]{:S(2)}) async-start(bf16[32,160,128]{2,1,0:T(8,128)(2,1)} %get-tuple-element.8), calls=%async_computation | async-start | bytes 2621440 | tf_op jit(solution)/shard_map/all_to_all | solution.py:303
  16.9 3.4 %collective-permute-start = (bf16[16,64,128]{2,1,0:T(8,128)(2,1)S(1)}, bf16[16,64,128]{2,1,0:T(8,128)(2,1)S(1)}, u32[]{:S(2)}, u32[]{:S(2)}) collective-permute-start(bf16[16,64,128]{2,1,0:T(8,128)(2,1)S(1)} %copy-done.3), channel_id=1, source_target_pairs={{0,16},{16,0},{32,48},{48,32},{64,80},{80,64},{96,112},{112,96},{1... | collective-permute-start | bytes 786440 | tf_op jit(solution)/shard_map/ppermute | solution.py:266
  20.4 17.6 %collective-permute-start.3 = (bf16[2,4,64,128]{3,2,1,0:T(8,128)(2,1)S(1)}, bf16[2,4,64,128]{3,2,1,0:T(8,128)(2,1)S(1)}, u32[]{:S(2)}, u32[]{:S(2)}) collective-permute-start(bf16[2,4,64,128]{3,2,1,0:T(8,128)(2,1)S(1)} %pad_maximum_fusion.4), channel_id=1, source_target_pairs={{0,384},{16,400},{32,416},{48,432},{64,448},{80,464},{96,480},{112... | collective-permute-start | bytes 393224 | tf_op jit(solution)/shard_map/ppermute | solution.py:266
  25.0 13.0 %collective-permute-start.2 = (bf16[2,4,64,128]{3,2,1,0:T(8,128)(2,1)S(1)}, bf16[2,4,64,128]{3,2,1,0:T(8,128)(2,1)S(1)}, u32[]{:S(2)}, u32[]{:S(2)}) collective-permute-start(bf16[2,4,64,128]{3,2,1,0:T(8,128)(2,1)S(1)} %pad_maximum_fusion.3), channel_id=1, source_target_pairs={{0,256},{16,272},{32,288},{48,304},{64,320},{80,336},{96,352},{112... | collective-permute-start | bytes 393224 | tf_op jit(solution)/shard_map/ppermute | solution.py:266
  27.4 11.8 %collective-permute-start.1 = (bf16[2,4,64,128]{3,2,1,0:T(8,128)(2,1)S(1)}, bf16[2,4,64,128]{3,2,1,0:T(8,128)(2,1)S(1)}, u32[]{:S(2)}, u32[]{:S(2)}) collective-permute-start(bf16[2,4,64,128]{3,2,1,0:T(8,128)(2,1)S(1)} %pad_maximum_fusion.2), channel_id=1, source_target_pairs={{0,128},{16,144},{32,160},{48,176},{64,192},{80,208},{96,224},{112... | collective-permute-start | bytes 393224 | tf_op jit(solution)/shard_map/ppermute | solution.py:266
  39.3 21.7 %collective-permute-start.4 = (bf16[2,4,64,128]{3,2,1,0:T(8,128)(2,1)S(1)}, bf16[2,4,64,128]{3,2,1,0:T(8,128)(2,1)S(1)}, u32[]{:S(2)}, u32[]{:S(2)}) collective-permute-start(bf16[2,4,64,128]{3,2,1,0:T(8,128)(2,1)S(1)} %pad_maximum_fusion.6), channel_id=1, source_target_pairs={{0,32},{16,48},{32,0},{48,16},{64,96},{80,112},{96,64},{112,80},{1... | collective-permute-start | bytes 393224 | tf_op jit(solution)/shard_map/ppermute | solution.py:266
  44.2 18.4 %collective-permute-start.5 = (bf16[2,4,64,128]{3,2,1,0:T(8,128)(2,1)S(1)}, bf16[2,4,64,128]{3,2,1,0:T(8,128)(2,1)S(1)}, u32[]{:S(2)}, u32[]{:S(2)}) collective-permute-start(bf16[2,4,64,128]{3,2,1,0:T(8,128)(2,1)S(1)} %pad_maximum_fusion.7), channel_id=1, source_target_pairs={{0,64},{16,80},{32,96},{48,112},{64,0},{80,16},{96,32},{112,48},{1... | collective-permute-start | bytes 393224 | tf_op jit(solution)/shard_map/ppermute | solution.py:266
  49.1 13.5 %collective-permute-start.6 = (bf16[2,4,64,128]{3,2,1,0:T(8,128)(2,1)S(1)}, bf16[2,4,64,128]{3,2,1,0:T(8,128)(2,1)S(1)}, u32[]{:S(2)}, u32[]{:S(2)}) collective-permute-start(bf16[2,4,64,128]{3,2,1,0:T(8,128)(2,1)S(1)} %fusion.3), channel_id=1, source_target_pairs={{0,96},{16,112},{32,64},{48,80},{64,32},{80,48},{96,0},{112,16},{1... | collective-permute-start | bytes 393224 | tf_op jit(solution)/shard_map/ppermute | solution.py:266
  51.5 5.6 %copy-start = (bf16[512,512]{1,0:T(8,128)(2,1)S(1)}, bf16[512,512]{1,0:T(8,128)(2,1)}, u32[]{:S(2)}) copy-start(bf16[512,512]{1,0:T(8,128)(2,1)} %constant.24.clone.fwd_ref) | copy-start | bytes 1572868
  51.5 5.6 %copy-start.1 = (bf16[2,256,512]{2,1,0:T(8,128)(2,1)S(1)}, bf16[2,256,512]{2,1,0:T(8,128)(2,1)}, u32[]{:S(2)}) copy-start(bf16[2,256,512]{2,1,0:T(8,128)(2,1)} %constant.25.clone.inv_ref) | copy-start | bytes 1572868

commit v5 on v4

--- a/solution.py
+++ b/solution.py
@@ -14,8 +14,9 @@
 TILE = 128
 VMEM_LIMIT = 48 * 1024 * 1024
 CHUNKS = 4
-CONV_COST = 1024
-RECURSE = False
+EARLY = 16
+ORDER_X = (0, 3, 2, 1)
+ORDER_Z = (0, 2, 3, 1)
 
 
 def bf16_parts(table, count):
@@ -64,23 +65,28 @@
     loads_v = []
     for head in range(heads):
         cols = pl.ds(head * HEAD_DIM, HEAD_DIM)
-        for place, ref in enumerate((x_ref, k_ref)):
-            step = copy(
-                ref.at[:, cols], held.at[head, pl.ds(place * tok, tok)], load.at[head // group]
-            )
+        parts = [
+            (x_ref.at[:, cols], pl.ds(0, tok)),
+            (k_ref.at[:, cols], pl.ds(tok, tok)),
+            (v_ref.at[pl.ds(0, EARLY), cols], pl.ds(2 * tok + part, EARLY)),
+        ]
+        for source, rows in parts:
+            step = copy(source, held.at[head, rows], load.at[head // group])
             step.start()
             loads[head // group].append(step)
     for head in range(heads):
         cols = pl.ds(head * HEAD_DIM, HEAD_DIM)
         apart = lax.bitwise_xor(me, jnp.int32(head))
         place = lax.bitwise_and(apart, 1) * (heads // 2) + lax.shift_right_logical(apart, 1)
-        step = copy(v_ref.at[:, cols], kept.at[place], load.at[CHUNKS + 1])
+        step = copy(
+            v_ref.at[pl.ds(EARLY, tok - EARLY), cols], kept.at[place], load.at[CHUNKS + 1]
+        )
         step.start()
         loads_v.append(step)
     filters.wait()
     for head in range(heads):
         first = head % 2 * part
-        held[head, 2 * tok :, :] = half[first : first + part, :]
+        held[head, 2 * tok : 2 * tok + part, :] = half[first : first + part, :]
     stores = []
     for chunk in range(CHUNKS):
         for step in loads[chunk]:
@@ -104,8 +110,8 @@
 def pack(me, hyena_in, keys, values, filt):
     tok, width = hyena_in.shape
     heads = width // HEAD_DIM
-    shape = (heads, 2 * tok + tok // 2, HEAD_DIM)
-    shape_v = (heads // 2, tok, HEAD_DIM)
+    shape = (heads, 2 * tok + tok // 2 + EARLY, HEAD_DIM)
+    shape_v = (heads // 2, tok - EARLY, HEAD_DIM)
     anywhere = pl.BlockSpec(memory_space=pl.ANY)
     return pl.pallas_call(
         pack_kernel,
@@ -114,7 +120,7 @@
         out_specs=[anywhere] * 3,
         scratch_shapes=[
             pltpu.VMEM(shape, jnp.bfloat16),
-            pltpu.VMEM((heads, tok, HEAD_DIM), jnp.bfloat16),
+            pltpu.VMEM((heads, tok - EARLY, HEAD_DIM), jnp.bfloat16),
             pltpu.VMEM((tok, HEAD_DIM), jnp.bfloat16),
             pltpu.SemaphoreType.DMA((CHUNKS + 2,)),
             pltpu.SemaphoreType.DMA((CHUNKS + 2,)),
@@ -126,55 +132,39 @@
     )(me, hyena_in, keys, values, filt)
 
 
+def spectra(halves, table, result):
+    width = result.shape[2]
+    rows = BLOCK // 2
+    first, second = halves
+    for pair in range(result.shape[0] // 2):
+        both = [
+            jnp.concatenate(
+                [half[block].reshape(rows, width) for block in (2 * pair, 2 * pair + 1)], axis=1
+            )
+            for half in (first, second)
+        ]
+        got = dot(table, jnp.concatenate(both + both, axis=0))
+        result[2 * pair] = got[:, :width]
+        result[2 * pair + 1] = got[:, width:]
+
+
 def conv_kernel(
-    me_ref,
-    y_ref,
-    other_ref,
-    fwd_ref,
-    inv_ref,
-    out_ref,
-    spec,
-    fspec,
-    filt,
-    bias,
-    queries,
+    y_ref, filt_ref, fwd_ref, inv_ref, out_ref, spec, fspec, bias, queries
 ):
     sources, _, width = y_ref.shape
-    half = other_ref.shape[1]
+    half = filt_ref.shape[2]
     tok = 2 * half
     per = BLOCK // tok
     blocks = sources // per
-    odd = lax.bitwise_and(me_ref[0], 1)
-    for source in range(sources):
-        at = pl.multiple_of(source * tok + (1 - odd) * half, half)
-        filt[pl.ds(at, half), :] = other_ref[source]
-    row = lax.broadcasted_iota(jnp.int32, (2 * TILE, TILE), 1)
-    col = lax.broadcasted_iota(jnp.int32, (2 * TILE, TILE), 0)
-    allowed = (col <= row + TILE) & (col >= row // tok * tok)
-    bias[...] = jnp.where(allowed, 0.0, -1e30)
-    for source in range(sources):
-        at = pl.multiple_of(source * tok + odd * half, half)
-        filt[pl.ds(at, half), :] = y_ref[source, 2 * tok :, :]
-
-    for pair in range(blocks // 2):
-        x_both = jnp.concatenate(
-            [
-                y_ref[block * per : (block + 1) * per, :tok, :].reshape(BLOCK, width)
-                for block in (2 * pair, 2 * pair + 1)
-            ],
-            axis=1,
-        )
-        f_both = jnp.concatenate(
-            [
-                filt[block * BLOCK : (block + 1) * BLOCK, :]
-                for block in (2 * pair, 2 * pair + 1)
-            ],
-            axis=1,
-        )
-        for both, result in ((x_both, spec), (f_both, fspec)):
-            got = dot(fwd_ref[...], jnp.concatenate([both, both], axis=0))
-            result[2 * pair] = got[:, :width]
-            result[2 * pair + 1] = got[:, width:]
+    groups = [slice(first, first + per) for first in range(0, sources, per)]
+    spectra(
+        [[y_ref[some, :half, :] for some in groups], [y_ref[some, half:tok, :] for some in groups]],
+        fwd_ref[...],
+        spec,
+    )
+    spectra(
+        [[filt_ref[part, some] for some in groups] for part in range(2)], fwd_ref[...], fspec
+    )
 
     sign = 1.0 - 2.0 * (lax.broadcasted_iota(jnp.int32, (8, width), 0) % 2).astype(jnp.float32)
 
@@ -218,6 +208,10 @@
 
     reach = TILE // tok
     factor = math.log2(math.e) / math.sqrt(HEAD_DIM)
+    row = lax.broadcasted_iota(jnp.int32, (2 * TILE, TILE), 1)
+    col = lax.broadcasted_iota(jnp.int32, (2 * TILE, TILE), 0)
+    allowed = (col <= row + TILE) & (col >= row // tok * tok)
+    bias[...] = jnp.where(allowed, 0.0, -1e30)
     for tile in range(sources // reach):
         first = max(tile * reach - reach, 0)
         last = (tile + 1) * reach
@@ -234,15 +228,17 @@
         out_ref[tile, 2 * TILE - span :, :] = probs.astype(jnp.bfloat16)
 
 
-def mix_kernel(me_ref, probs_ref, *refs):
+def mix_kernel(me_ref, probs_ref, y_ref, *refs):
     pieces, out_ref, val = refs[:-2], refs[-2], refs[-1]
     sources, tok, width = val.shape
     me = me_ref[0]
+    for source in range(sources):
+        val[source, :EARLY, :] = y_ref[source, 2 * tok + tok // 2 :, :]
     for along_z, ref in enumerate(pieces):
         for core in range(2):
             for along_x in range(ref.shape[1]):
-                apart = along_x * 8 + along_z * 2 + core
-                val[lax.bitwise_xor(me, jnp.int32(apart))] = ref[core, along_x]
+                apart = ORDER_X[along_x] * 8 + ORDER_Z[along_z] * 2 + core
+                val[lax.bitwise_xor(me, jnp.int32(apart)), EARLY:, :] = ref[core, along_x]
     reach = TILE // tok
     for tile in range(sources // reach):
         first = max(tile * reach - reach, 0)
@@ -270,19 +266,13 @@
     _, tok, width = near.shape
     near = near.reshape(4, 4, tok, width)
     other = swap(far, 1).reshape(4, 4, tok, width)
-    if RECURSE:
-        both = jnp.stack([near, other])
-        step = swap(jnp.stack([both[:, 1], both[:, 3]]), 8)
-        last = swap(jnp.stack([both[:, 2], step[1]]), 16)
-        arrived = [both[:, 0], step[0], last[0], last[1]]
-    else:
-        arrived = []
-        for along_x in range(4):
-            both = jnp.stack([near[along_x], other[along_x]])
-            arrived.append(swap(both, along_x * 8) if along_x else both)
+    arrived = []
+    for along_x in range(4):
+        both = jnp.stack([near[along_x], other[along_x]])
+        arrived.append(swap(both, along_x * 8) if along_x else both)
     pieces = []
-    for along_z in range(4):
-        mine = jnp.stack([some[:, along_z] for some in arrived], axis=1)
+    for along_z in ORDER_Z:
+        mine = jnp.stack([arrived[x][:, along_z] for x in ORDER_X], axis=1)
         pieces.append(swap(mine, along_z * 2) if along_z else mine)
     return pieces
 
@@ -293,7 +283,9 @@
     blocks = peers * tok // BLOCK
     tiles = peers * tok // TILE
     hi, lo = bf16_parts(forward_table(), 2)
-    fwd = jnp.asarray(np.concatenate([hi, lo], axis=1))
+    place = np.arange(BLOCK) % tok // (tok // 2)
+    order = np.concatenate([np.flatnonzero(place == 0), np.flatnonzero(place == 1)])
+    fwd = jnp.asarray(np.concatenate([hi[:, order], lo[:, order]], axis=1))
     inv = jnp.asarray(bf16_parts(inverse_table(), 2))
     me = lax.axis_index("context").astype(jnp.int32).reshape(1)
     params = pltpu.CompilerParams(vmem_limit_bytes=VMEM_LIMIT)
@@ -302,37 +294,35 @@
     packed, near, far = pack(me, hyena_in, keys, values, filt)
     moved = lax.all_to_all(packed, "context", split_axis=0, concat_axis=0, tiled=True)
     pieces = route(near, far)
-    mine = moved[:, 2 * tok :]
+    half = moved[:, 2 * tok : 2 * tok + tok // 2]
     pairs = [[i, i + 1] for i in range(0, peers, 2)]
-    both = lax.all_to_all(jnp.stack([mine, mine]), "context", 0, 0, axis_index_groups=pairs, tiled=True)
-    other = jnp.where(me[0] % 2 == 1, both[0], both[1])
+    filters = lax.all_gather(half, "context", axis_index_groups=pairs, axis=0, tiled=False)
 
     probs = pl.pallas_call(
         conv_kernel,
         out_shape=jax.ShapeDtypeStruct((tiles, 2 * TILE, TILE), jnp.bfloat16),
-        in_specs=[scalar] + vmem(4),
+        in_specs=vmem(4),
         out_specs=vmem(1)[0],
         scratch_shapes=[
             pltpu.VMEM((blocks, 2 * BLOCK, HEAD_DIM), jnp.float32),
             pltpu.VMEM((blocks, 2 * BLOCK, HEAD_DIM), jnp.float32),
-            pltpu.VMEM((peers * tok, HEAD_DIM), jnp.bfloat16),
             pltpu.VMEM((2 * TILE, TILE), jnp.float32),
             pltpu.VMEM((peers * tok, HEAD_DIM), jnp.bfloat16),
         ],
         compiler_params=params,
         cost_estimate=pl.CostEstimate(flops=5 << 30, bytes_accessed=5 << 20, transcendentals=1 << 19),
         name="conv_probs",
-    )(me, moved, other, fwd, inv)
+    )(moved, filters, fwd, inv)
     mixed = pl.pallas_call(
         mix_kernel,
         out_shape=jax.ShapeDtypeStruct((peers, tok, HEAD_DIM), jnp.bfloat16),
-        in_specs=[scalar] + vmem(5),
+        in_specs=[scalar] + vmem(6),
         out_specs=vmem(1)[0],
         scratch_shapes=[pltpu.VMEM((peers, tok, HEAD_DIM), jnp.bfloat16)],
         compiler_params=params,
         cost_estimate=pl.CostEstimate(flops=1 << 28, bytes_accessed=2 << 20, transcendentals=0),
         name="mix",
-    )(me, probs, *pieces)
+    )(me, probs, moved, *pieces)
     home = lax.all_to_all(mixed, "context", split_axis=0, concat_axis=0, tiled=True)
     return home.transpose(1, 0, 2).reshape(tok, width)
 

time: 89.1 us -> 87 us (0.976)
  blocking collectives: 30.2 us -> 26.3 us
  waiting for transfers between devices: 12.6 us -> 13.8 us
    all_to_all x1 -> x0, blocking collectives: 5.54 us -> none  [local(): lax.all_to_all(jnp.stack([mine, mine]), 'context', 0, 0, axis_index_group...]
    all_gather x0 -> x1, blocking collectives: none -> 2.89 us  [local(): lax.all_gather(half, 'context', axis_index_groups=pairs, axis=0, tiled=Fa...]
    ppermute x7, waiting for transfers between devices: 12.6 us -> 13.8 us  [swap(): return lax.ppermute(array, 'context', [(i, i ^ bits) for i in range(peers)])]
    all_to_all x1, blocking collectives: 24.6 us -> 23.4 us  [local(): lax.all_to_all(mixed, 'context', split_axis=0, concat_axis=0, tiled=True)]
  transfers between devices with their start and end apart: 8 -> 8, of which waited for: 4 -> 5; matrix products, arithmetic and copies ran while one was open for 0% -> 0% of each run, Pallas kernels for 4% -> 4%
where the time goes in v5:
time: 87 us; the launch traced here: 86.4 us
  starting transfers between devices  38.5 us (44%)
  blocking collectives  26.3 us (30%)
  waiting for transfers between devices  13.8 us (16%)
  Pallas kernels  6.49 us (7%)
  local copies, waits for them, and re-layouts  0.96 us (1%)
    ppermute x7, starting transfers between devices, swap(): return lax.ppermute(array, 'context', [(i, i ^ bits) for i in range(peers)])  24 us
    all_to_all x1, blocking collectives, local(): lax.all_to_all(mixed, 'context', split_axis=0, concat_axis=0, tiled=True)  23.4 us
    all_to_all x1, starting transfers between devices, local(): lax.all_to_all(packed, 'context', split_axis=0, concat_axis=0, tiled=True)  14.6 us
    ppermute x7, waiting for transfers between devices, swap(): return lax.ppermute(array, 'context', [(i, i ^ bits) for i in range(peers)])  13.8 us
    pallas_call x1, Pallas kernels, local(): pl.pallas_call(conv_kernel, out_shape=jax.ShapeDtypeStruct((tiles, 2 * TI...  3.68 us
    all_gather x1, blocking collectives, local(): lax.all_gather(half, 'context', axis_index_groups=pairs, axis=0, tiled=Fa...  2.89 us
    pallas_call x1, Pallas kernels, pack(): pl.pallas_call(pack_kernel, out_shape=[jax.ShapeDtypeStruct(some, jnp.bfl...  2.32 us
  transfers between devices with their start and end apart: 8, of which 5 were waited for; matrix products, arithmetic and copies ran while one was open for 0% of the time, Pallas kernels for 4%

profile of v5, /device:TPU:1, one launch (start us, length us, event | category | flops | bytes accessed | tf_op | source)
XLA Modules:
  0.0 86.4 jit_solution(823907143967719637)
XLA Ops:
  0.0 2.3 %pack.1 = (bf16[32,176,128]{2,1,0:T(8,128)(2,1)}, bf16[16,48,128]{2,1,0:T(8,128)(2,1)}, bf16[16,48,128]{2,1,0:T(8,128)(2,1)}) custom-call(s32[1]{0:T(128)} %bitcast.me_ref, bf16[64,4096]{1,0:T(8,128)(2,1)} %x_ref.1, bf16[64,4096]{1,0:T(8,128)(2,1)} %k_ref.1, bf16[64,4096]{1,0:T(8,128)(2,1)} %v_ref.1, bf16[64,128]{1,0:T(8,128)(2,1)} %f_ref.1), custom_call_target="tpu_custom_call" | custom-call | bytes 3670016 | tf_op jit(solution)/shard_map/pack/pallas_call | solution.py:116
  2.3 0.0 copy-start.3
  2.3 0.0 copy-start.2
  2.4 14.6 %all-to-all-start = ((bf16[32,176,128]{2,1,0:T(8,128)(2,1)}), bf16[32,176,128]{2,1,0:T(8,128)(2,1)S(1)}, u32[]{:S(2)}, u32[]{:S(2)}) async-start(bf16[32,176,128]{2,1,0:T(8,128)(2,1)} %get-tuple-element.8), calls=%async_computation | async-start | bytes 2883584 | tf_op jit(solution)/shard_map/all_to_all | solution.py:295
  16.9 0.0 copy-done.3
  16.9 2.1 %collective-permute-start = (bf16[16,48,128]{2,1,0:T(8,128)(2,1)S(1)}, bf16[16,48,128]{2,1,0:T(8,128)(2,1)S(1)}, u32[]{:S(2)}, u32[]{:S(2)}) collective-permute-start(bf16[16,48,128]{2,1,0:T(8,128)(2,1)S(1)} %copy-done.3), channel_id=1, source_target_pairs={{0,16},{16,0},{32,48},{48,32},{64,80},{80,64},{96,112},{112,96},{1... | collective-permute-start | bytes 589832 | tf_op jit(solution)/shard_map/ppermute | solution.py:262
  19.1 0.0 copy-done.2
  19.1 1.1 %collective-permute-done = bf16[16,48,128]{2,1,0:T(8,128)(2,1)S(1)} collective-permute-done((bf16[16,48,128]{2,1,0:T(8,128)(2,1)S(1)}, bf16[16,48,128]{2,1,0:T(8,128)(2,1)S(1)}, u32[]{:S(2)}, u32[]{:S(2)}) %collective-permute-start) | collective-permute-done | bytes 196640 | tf_op jit(solution)/shard_map/ppermute | solution.py:262
  20.3 4.5 %collective-permute-start.1 = (bf16[2,4,48,128]{3,2,1,0:T(8,128)(2,1)S(1)}, bf16[2,4,48,128]{3,2,1,0:T(8,128)(2,1)S(1)}, u32[]{:S(2)}, u32[]{:S(2)}) collective-permute-start(bf16[2,4,48,128]{3,2,1,0:T(8,128)(2,1)S(1)} %pad_maximum_fusion), channel_id=1, source_target_pairs={{0,384},{16,400},{32,416},{48,432},{64,448},{80,464},{96,480},{112... | collective-permute-start | bytes 294920 | tf_op jit(solution)/shard_map/ppermute | solution.py:262
  24.9 2.4 %collective-permute-start.2 = (bf16[2,4,48,128]{3,2,1,0:T(8,128)(2,1)S(1)}, bf16[2,4,48,128]{3,2,1,0:T(8,128)(2,1)S(1)}, u32[]{:S(2)}, u32[]{:S(2)}) collective-permute-start(bf16[2,4,48,128]{3,2,1,0:T(8,128)(2,1)S(1)} %pad_maximum_fusion.1), channel_id=1, source_target_pairs={{0,256},{16,272},{32,288},{48,304},{64,320},{80,336},{96,352},{112... | collective-permute-start | bytes 294920 | tf_op jit(solution)/shard_map/ppermute | solution.py:262
  27.4 2.0 %collective-permute-start.3 = (bf16[2,4,48,128]{3,2,1,0:T(8,128)(2,1)S(1)}, bf16[2,4,48,128]{3,2,1,0:T(8,128)(2,1)S(1)}, u32[]{:S(2)}, u32[]{:S(2)}) collective-permute-start(bf16[2,4,48,128]{3,2,1,0:T(8,128)(2,1)S(1)} %pad_maximum_fusion.2), channel_id=1, source_target_pairs={{0,128},{16,144},{32,160},{48,176},{64,192},{80,208},{96,224},{112... | collective-permute-start | bytes 294920 | tf_op jit(solution)/shard_map/ppermute | solution.py:262
  29.4 0.0 copy-start
  29.4 0.0 copy-start.1
  29.4 5.0 %collective-permute-done.1 = bf16[2,4,48,128]{3,2,1,0:T(8,128)(2,1)S(1)} collective-permute-done((bf16[2,4,48,128]{3,2,1,0:T(8,128)(2,1)S(1)}, bf16[2,4,48,128]{3,2,1,0:T(8,128)(2,1)S(1)}, u32[]{:S(2)}, u32[]{:S(2)}) %collective-permute-start.1) | collective-permute-done | bytes 98336 | tf_op jit(solution)/shard_map/ppermute | solution.py:262
  34.4 0.0 collective-permute-done.2
  34.4 2.0 %collective-permute-done.3 = bf16[2,4,48,128]{3,2,1,0:T(8,128)(2,1)S(1)} collective-permute-done((bf16[2,4,48,128]{3,2,1,0:T(8,128)(2,1)S(1)}, bf16[2,4,48,128]{3,2,1,0:T(8,128)(2,1)S(1)}, u32[]{:S(2)}, u32[]{:S(2)}) %collective-permute-start.3) | collective-permute-done | bytes 98336 | tf_op jit(solution)/shard_map/ppermute | solution.py:262
  36.4 8.7 %collective-permute-start.4 = (bf16[2,4,48,128]{3,2,1,0:T(8,128)(2,1)S(1)}, bf16[2,4,48,128]{3,2,1,0:T(8,128)(2,1)S(1)}, u32[]{:S(2)}, u32[]{:S(2)}) collective-permute-start(bf16[2,4,48,128]{3,2,1,0:T(8,128)(2,1)S(1)} %pad_maximum_fusion.4), channel_id=1, source_target_pairs={{0,64},{16,80},{32,96},{48,112},{64,0},{80,16},{96,32},{112,48},{1... | collective-permute-start | bytes 294920 | tf_op jit(solution)/shard_map/ppermute | solution.py:262
  45.2 1.9 %collective-permute-start.5 = (bf16[2,4,48,128]{3,2,1,0:T(8,128)(2,1)S(1)}, bf16[2,4,48,128]{3,2,1,0:T(8,128)(2,1)S(1)}, u32[]{:S(2)}, u32[]{:S(2)}) collective-permute-start(bf16[2,4,48,128]{3,2,1,0:T(8,128)(2,1)S(1)} %pad_maximum_fusion.5), channel_id=1, source_target_pairs={{0,96},{16,112},{32,64},{48,80},{64,32},{80,48},{96,0},{112,16},{1... | collective-permute-start | bytes 294920 | tf_op jit(solution)/shard_map/ppermute | solution.py:262
  47.1 2.2 %collective-permute-start.6 = (bf16[2,4,48,128]{3,2,1,0:T(8,128)(2,1)S(1)}, bf16[2,4,48,128]{3,2,1,0:T(8,128)(2,1)S(1)}, u32[]{:S(2)}, u32[]{:S(2)}) collective-permute-start(bf16[2,4,48,128]{3,2,1,0:T(8,128)(2,1)S(1)} %fusion.5), channel_id=1, source_target_pairs={{0,32},{16,48},{32,0},{48,16},{64,96},{80,112},{96,64},{112,80},{1... | collective-permute-start | bytes 294920 | tf_op jit(solution)/shard_map/ppermute | solution.py:262
  49.3 0.0 all-to-all-done.y_ref
  49.4 2.9 %all-gather = bf16[64,32,128]{2,1,0:T(8,128)(2,1)S(1)} all-gather(bf16[32,32,128]{2,1,0:T(8,128)(2,1)S(1)} %slice.132), channel_id=2, replica_groups={{0,16},{32,48},{64,80},{96,112},{128,144},{160,176},{192,208},{224,240}..., dimensions={0}, use_global_device_ids=true | all-gather | bytes 786432 | tf_op jit(solution)/shard_map/all_gather | solution.py:299
  52.3 0.0 copy-done
  52.3 0.0 copy-done.1
  52.3 3.7 %conv_probs.1.probs_ref = bf16[16,256,128]{2,1,0:T(8,128)(2,1)S(1)} custom-call(bf16[32,176,128]{2,1,0:T(8,128)(2,1)S(1)} %all-to-all-done.y_ref, bf16[2,32,32,128]{3,2,1,0:T(8,128)(2,1)S(1)} %bitcast.24, bf16[512,512]{1,0:T(8,128)(2,1)S(1)} %copy-done.1, bf16[2,256,512]{2,1,0:T(8,128)(2,1)S(1)} %copy-done), custom_call_target="tpu_custom_call" | custom-call | flops 5368709120 | bytes 5242880 | tf_op jit(solution)/shard_map/conv_probs/pallas_call | solution.py:301
  56.0 4.4 %collective-permute-done.4.refs_1_ = bf16[2,4,48,128]{3,2,1,0:T(8,128)(2,1)S(1)} collective-permute-done((bf16[2,4,48,128]{3,2,1,0:T(8,128)(2,1)S(1)}, bf16[2,4,48,128]{3,2,1,0:T(8,128)(2,1)S(1)}, u32[]{:S(2)}, u32[]{:S(2)}) %collective-permute-start.4) | collective-permute-done | bytes 98336 | tf_op jit(solution)/shard_map/ppermute | solution.py:262
  60.4 1.3 %collective-permute-done.5.refs_2_ = bf16[2,4,48,128]{3,2,1,0:T(8,128)(2,1)S(1)} collective-permute-done((bf16[2,4,48,128]{3,2,1,0:T(8,128)(2,1)S(1)}, bf16[2,4,48,128]{3,2,1,0:T(8,128)(2,1)S(1)}, u32[]{:S(2)}, u32[]{:S(2)}) %collective-permute-start.5) | collective-permute-done | bytes 98336 | tf_op jit(solution)/shard_map/ppermute | solution.py:262
  61.7 0.0 collective-permute-done.6.refs_3_
  61.7 0.5 mix.1
  62.2 23.4 %all_to_all.10 = bf16[32,64,128]{2,1,0:T(8,128)(2,1)S(1)} all-to-all(bf16[32,64,128]{2,1,0:T(8,128)(2,1)S(1)} %mix.1), channel_id=1, replica_groups=mesh['context'=32,'dp'=16] {'context'}, dimensions={0} | all-to-all | bytes 1048576 | tf_op jit(solution)/shard_map/all_to_all | solution.py:326
  85.6 0.9 copy_bitcast_fusion
  (14 shorter events, 0.2 us)
Async XLA Ops:
  2.3 14.6 %copy-start.3 = (bf16[16,48,128]{2,1,0:T(8,128)(2,1)S(1)}, bf16[16,48,128]{2,1,0:T(8,128)(2,1)}, u32[]{:S(2)}) copy-start(bf16[16,48,128]{2,1,0:T(8,128)(2,1)} %get-tuple-element.10) | copy-start | bytes 589828
  2.3 16.8 %copy-start.2 = (bf16[16,48,128]{2,1,0:T(8,128)(2,1)S(1)}, bf16[16,48,128]{2,1,0:T(8,128)(2,1)}, u32[]{:S(2)}) copy-start(bf16[16,48,128]{2,1,0:T(8,128)(2,1)} %get-tuple-element.9) | copy-start | bytes 589828
  2.4 47.0 %all-to-all-start = ((bf16[32,176,128]{2,1,0:T(8,128)(2,1)}), bf16[32,176,128]{2,1,0:T(8,128)(2,1)S(1)}, u32[]{:S(2)}, u32[]{:S(2)}) async-start(bf16[32,176,128]{2,1,0:T(8,128)(2,1)} %get-tuple-element.8), calls=%async_computation | async-start | bytes 2883584 | tf_op jit(solution)/shard_map/all_to_all | solution.py:295
  16.9 3.3 %collective-permute-start = (bf16[16,48,128]{2,1,0:T(8,128)(2,1)S(1)}, bf16[16,48,128]{2,1,0:T(8,128)(2,1)S(1)}, u32[]{:S(2)}, u32[]{:S(2)}) collective-permute-start(bf16[16,48,128]{2,1,0:T(8,128)(2,1)S(1)} %copy-done.3), channel_id=1, source_target_pairs={{0,16},{16,0},{32,48},{48,32},{64,80},{80,64},{96,112},{112,96},{1... | collective-permute-start | bytes 589832 | tf_op jit(solution)/shard_map/ppermute | solution.py:262
  20.3 14.1 %collective-permute-start.1 = (bf16[2,4,48,128]{3,2,1,0:T(8,128)(2,1)S(1)}, bf16[2,4,48,128]{3,2,1,0:T(8,128)(2,1)S(1)}, u32[]{:S(2)}, u32[]{:S(2)}) collective-permute-start(bf16[2,4,48,128]{3,2,1,0:T(8,128)(2,1)S(1)} %pad_maximum_fusion), channel_id=1, source_target_pairs={{0,384},{16,400},{32,416},{48,432},{64,448},{80,464},{96,480},{112... | collective-permute-start | bytes 294920 | tf_op jit(solution)/shard_map/ppermute | solution.py:262
  24.9 9.5 %collective-permute-start.2 = (bf16[2,4,48,128]{3,2,1,0:T(8,128)(2,1)S(1)}, bf16[2,4,48,128]{3,2,1,0:T(8,128)(2,1)S(1)}, u32[]{:S(2)}, u32[]{:S(2)}) collective-permute-start(bf16[2,4,48,128]{3,2,1,0:T(8,128)(2,1)S(1)} %pad_maximum_fusion.1), channel_id=1, source_target_pairs={{0,256},{16,272},{32,288},{48,304},{64,320},{80,336},{96,352},{112... | collective-permute-start | bytes 294920 | tf_op jit(solution)/shard_map/ppermute | solution.py:262
  27.4 9.0 %collective-permute-start.3 = (bf16[2,4,48,128]{3,2,1,0:T(8,128)(2,1)S(1)}, bf16[2,4,48,128]{3,2,1,0:T(8,128)(2,1)S(1)}, u32[]{:S(2)}, u32[]{:S(2)}) collective-permute-start(bf16[2,4,48,128]{3,2,1,0:T(8,128)(2,1)S(1)} %pad_maximum_fusion.2), channel_id=1, source_target_pairs={{0,128},{16,144},{32,160},{48,176},{64,192},{80,208},{96,224},{112... | collective-permute-start | bytes 294920 | tf_op jit(solution)/shard_map/ppermute | solution.py:262
  29.4 22.9 %copy-start = (bf16[2,256,512]{2,1,0:T(8,128)(2,1)S(1)}, bf16[2,256,512]{2,1,0:T(8,128)(2,1)}, u32[]{:S(2)}) copy-start(bf16[2,256,512]{2,1,0:T(8,128)(2,1)} %constant.11.clone.inv_ref) | copy-start | bytes 1572868
  29.4 22.9 %copy-start.1 = (bf16[512,512]{1,0:T(8,128)(2,1)S(1)}, bf16[512,512]{1,0:T(8,128)(2,1)}, u32[]{:S(2)}) copy-start(bf16[512,512]{1,0:T(8,128)(2,1)} %constant.10.clone.fwd_ref) | copy-start | bytes 1572868
  36.4 24.0 %collective-permute-start.4 = (bf16[2,4,48,128]{3,2,1,0:T(8,128)(2,1)S(1)}, bf16[2,4,48,128]{3,2,1,0:T(8,128)(2,1)S(1)}, u32[]{:S(2)}, u32[]{:S(2)}) collective-permute-start(bf16[2,4,48,128]{3,2,1,0:T(8,128)(2,1)S(1)} %pad_maximum_fusion.4), channel_id=1, source_target_pairs={{0,64},{16,80},{32,96},{48,112},{64,0},{80,16},{96,32},{112,48},{1... | collective-permute-start | bytes 294920 | tf_op jit(solution)/shard_map/ppermute | solution.py:262
  45.2 16.5 %collective-permute-start.5 = (bf16[2,4,48,128]{3,2,1,0:T(8,128)(2,1)S(1)}, bf16[2,4,48,128]{3,2,1,0:T(8,128)(2,1)S(1)}, u32[]{:S(2)}, u32[]{:S(2)}) collective-permute-start(bf16[2,4,48,128]{3,2,1,0:T(8,128)(2,1)S(1)} %pad_maximum_fusion.5), channel_id=1, source_target_pairs={{0,96},{16,112},{32,64},{48,80},{64,32},{80,48},{96,0},{112,16},{1... | collective-permute-start | bytes 294920 | tf_op jit(solution)/shard_map/ppermute | solution.py:262
  47.1 14.6 %collective-permute-start.6 = (bf16[2,4,48,128]{3,2,1,0:T(8,128)(2,1)S(1)}, bf16[2,4,48,128]{3,2,1,0:T(8,128)(2,1)S(1)}, u32[]{:S(2)}, u32[]{:S(2)}) collective-permute-start(bf16[2,4,48,128]{3,2,1,0:T(8,128)(2,1)S(1)} %fusion.5), channel_id=1, source_target_pairs={{0,32},{16,48},{32,0},{48,16},{64,96},{80,112},{96,64},{112,80},{1... | collective-permute-start | bytes 294920 | tf_op jit(solution)/shard_map/ppermute | solution.py:262

commit v6 on v5

--- a/solution.py
+++ b/solution.py
@@ -57,7 +57,7 @@
     tok, width = x_ref.shape
     heads = width // HEAD_DIM
     group = heads // CHUNKS
-    part = tok // 2
+    part = tok // 4
     me = me_ref[0]
     filters = copy(f_ref, half, load.at[CHUNKS])
     filters.start()
@@ -85,7 +85,7 @@
         loads_v.append(step)
     filters.wait()
     for head in range(heads):
-        first = head % 2 * part
+        first = (head // 8 % 2 * 2 + head % 2) * part
         held[head, 2 * tok : 2 * tok + part, :] = half[first : first + part, :]
     stores = []
     for chunk in range(CHUNKS):
@@ -110,7 +110,7 @@
 def pack(me, hyena_in, keys, values, filt):
     tok, width = hyena_in.shape
     heads = width // HEAD_DIM
-    shape = (heads, 2 * tok + tok // 2 + EARLY, HEAD_DIM)
+    shape = (heads, 2 * tok + tok // 4 + EARLY, HEAD_DIM)
     shape_v = (heads // 2, tok - EARLY, HEAD_DIM)
     anywhere = pl.BlockSpec(memory_space=pl.ANY)
     return pl.pallas_call(
@@ -134,14 +134,13 @@
 
 def spectra(halves, table, result):
     width = result.shape[2]
-    rows = BLOCK // 2
-    first, second = halves
+    rows = BLOCK // len(halves)
     for pair in range(result.shape[0] // 2):
         both = [
             jnp.concatenate(
                 [half[block].reshape(rows, width) for block in (2 * pair, 2 * pair + 1)], axis=1
             )
-            for half in (first, second)
+            for half in halves
         ]
         got = dot(table, jnp.concatenate(both + both, axis=0))
         result[2 * pair] = got[:, :width]
@@ -152,19 +151,17 @@
     y_ref, filt_ref, fwd_ref, inv_ref, out_ref, spec, fspec, bias, queries
 ):
     sources, _, width = y_ref.shape
-    half = filt_ref.shape[2]
-    tok = 2 * half
+    part = filt_ref.shape[2]
+    tok = 4 * part
     per = BLOCK // tok
     blocks = sources // per
     groups = [slice(first, first + per) for first in range(0, sources, per)]
     spectra(
-        [[y_ref[some, :half, :] for some in groups], [y_ref[some, half:tok, :] for some in groups]],
+        [[y_ref[some, q * part : (q + 1) * part, :] for some in groups] for q in range(4)],
         fwd_ref[...],
         spec,
     )
-    spectra(
-        [[filt_ref[part, some] for some in groups] for part in range(2)], fwd_ref[...], fspec
-    )
+    spectra([[filt_ref[q, some] for some in groups] for q in range(4)], fwd_ref[...], fspec)
 
     sign = 1.0 - 2.0 * (lax.broadcasted_iota(jnp.int32, (8, width), 0) % 2).astype(jnp.float32)
 
@@ -233,7 +230,7 @@
     sources, tok, width = val.shape
     me = me_ref[0]
     for source in range(sources):
-        val[source, :EARLY, :] = y_ref[source, 2 * tok + tok // 2 :, :]
+        val[source, :EARLY, :] = y_ref[source, 2 * tok + tok // 4 :, :]
     for along_z, ref in enumerate(pieces):
         for core in range(2):
             for along_x in range(ref.shape[1]):
@@ -283,8 +280,8 @@
     blocks = peers * tok // BLOCK
     tiles = peers * tok // TILE
     hi, lo = bf16_parts(forward_table(), 2)
-    place = np.arange(BLOCK) % tok // (tok // 2)
-    order = np.concatenate([np.flatnonzero(place == 0), np.flatnonzero(place == 1)])
+    place = np.arange(BLOCK) % tok // (tok // 4)
+    order = np.concatenate([np.flatnonzero(place == q) for q in range(4)])
     fwd = jnp.asarray(np.concatenate([hi[:, order], lo[:, order]], axis=1))
     inv = jnp.asarray(bf16_parts(inverse_table(), 2))
     me = lax.axis_index("context").astype(jnp.int32).reshape(1)
@@ -294,9 +291,9 @@
     packed, near, far = pack(me, hyena_in, keys, values, filt)
     moved = lax.all_to_all(packed, "context", split_axis=0, concat_axis=0, tiled=True)
     pieces = route(near, far)
-    half = moved[:, 2 * tok : 2 * tok + tok // 2]
-    pairs = [[i, i + 1] for i in range(0, peers, 2)]
-    filters = lax.all_gather(half, "context", axis_index_groups=pairs, axis=0, tiled=False)
+    quarter = moved[:, 2 * tok : 2 * tok + tok // 4]
+    fours = [[i, i + 1, i + 8, i + 9] for i in range(0, peers, 2) if i // 8 % 2 == 0]
+    filters = lax.all_gather(quarter, "context", axis_index_groups=fours, axis=0, tiled=False)
 
     probs = pl.pallas_call(
         conv_kernel,

time: 87 us -> 89.9 us (1.033)
  blocking collectives: 26.3 us -> 36 us
  waiting for transfers between devices: 13.8 us -> 7.7 us
    all_gather x1, blocking collectives: 2.89 us -> 10.2 us  [local(): lax.all_gather(quarter, 'context', axis_index_groups=fours, axis=0, tiled...]
    ppermute x7, waiting for transfers between devices: 13.8 us -> 7.7 us  [swap(): return lax.ppermute(array, 'context', [(i, i ^ bits) for i in range(peers)])]
    all_to_all x1, blocking collectives: 23.4 us -> 25.9 us  [local(): lax.all_to_all(mixed, 'context', split_axis=0, concat_axis=0, tiled=True)]
  transfers between devices with their start and end apart: 8 -> 8, of which waited for: 5 -> 3; matrix products, arithmetic and copies ran while one was open for 0% -> 0% of each run, Pallas kernels for 4% -> 4%
where the time goes in v6:
time: 89.9 us; the launch traced here: 89.3 us
  starting transfers between devices  37.8 us (42%)
  blocking collectives  36 us (40%)
  waiting for transfers between devices  7.7 us (9%)
  Pallas kernels  6.51 us (7%)
  local copies, waits for them, and re-layouts  0.95 us (1%)
    all_to_all x1, blocking collectives, local(): lax.all_to_all(mixed, 'context', split_axis=0, concat_axis=0, tiled=True)  25.9 us
    ppermute x7, starting transfers between devices, swap(): return lax.ppermute(array, 'context', [(i, i ^ bits) for i in range(peers)])  23.2 us
    all_to_all x1, starting transfers between devices, local(): lax.all_to_all(packed, 'context', split_axis=0, concat_axis=0, tiled=True)  14.6 us
    all_gather x1, blocking collectives, local(): lax.all_gather(quarter, 'context', axis_index_groups=fours, axis=0, tiled...  10.2 us
    ppermute x7, waiting for transfers between devices, swap(): return lax.ppermute(array, 'context', [(i, i ^ bits) for i in range(peers)])  7.7 us
    pallas_call x1, Pallas kernels, local(): pl.pallas_call(conv_kernel, out_shape=jax.ShapeDtypeStruct((tiles, 2 * TI...  3.68 us
    pallas_call x1, Pallas kernels, pack(): pl.pallas_call(pack_kernel, out_shape=[jax.ShapeDtypeStruct(some, jnp.bfl...  2.33 us
  transfers between devices with their start and end apart: 8, of which 3 were waited for; matrix products, arithmetic and copies ran while one was open for 0% of the time, Pallas kernels for 4%

profile of v6, /device:TPU:1, one launch (start us, length us, event | category | flops | bytes accessed | tf_op | source)
XLA Modules:
  0.0 89.3 jit_solution(2808295283449679125)
XLA Ops:
  0.0 2.3 %pack.1 = (bf16[32,160,128]{2,1,0:T(8,128)(2,1)}, bf16[16,48,128]{2,1,0:T(8,128)(2,1)}, bf16[16,48,128]{2,1,0:T(8,128)(2,1)}) custom-call(s32[1]{0:T(128)} %bitcast.me_ref, bf16[64,4096]{1,0:T(8,128)(2,1)} %x_ref.1, bf16[64,4096]{1,0:T(8,128)(2,1)} %k_ref.1, bf16[64,4096]{1,0:T(8,128)(2,1)} %v_ref.1, bf16[64,128]{1,0:T(8,128)(2,1)} %f_ref.1), custom_call_target="tpu_custom_call" | custom-call | bytes 3670016 | tf_op jit(solution)/shard_map/pack/pallas_call | solution.py:116
  2.3 0.0 copy-start.3
  2.4 0.0 copy-start.2
  2.4 14.6 %all-to-all-start = ((bf16[32,160,128]{2,1,0:T(8,128)(2,1)}), bf16[32,160,128]{2,1,0:T(8,128)(2,1)S(1)}, u32[]{:S(2)}, u32[]{:S(2)}) async-start(bf16[32,160,128]{2,1,0:T(8,128)(2,1)} %get-tuple-element.8), calls=%async_computation | async-start | bytes 2621440 | tf_op jit(solution)/shard_map/all_to_all | solution.py:292
  16.9 0.0 copy-done.3
  16.9 2.1 %collective-permute-start = (bf16[16,48,128]{2,1,0:T(8,128)(2,1)S(1)}, bf16[16,48,128]{2,1,0:T(8,128)(2,1)S(1)}, u32[]{:S(2)}, u32[]{:S(2)}) collective-permute-start(bf16[16,48,128]{2,1,0:T(8,128)(2,1)S(1)} %copy-done.3), channel_id=1, source_target_pairs={{0,16},{16,0},{32,48},{48,32},{64,80},{80,64},{96,112},{112,96},{1... | collective-permute-start | bytes 589832 | tf_op jit(solution)/shard_map/ppermute | solution.py:259
  19.1 0.0 copy-done.2
  19.1 1.1 %collective-permute-done = bf16[16,48,128]{2,1,0:T(8,128)(2,1)S(1)} collective-permute-done((bf16[16,48,128]{2,1,0:T(8,128)(2,1)S(1)}, bf16[16,48,128]{2,1,0:T(8,128)(2,1)S(1)}, u32[]{:S(2)}, u32[]{:S(2)}) %collective-permute-start) | collective-permute-done | bytes 196640 | tf_op jit(solution)/shard_map/ppermute | solution.py:259
  20.3 4.5 %collective-permute-start.1 = (bf16[2,4,48,128]{3,2,1,0:T(8,128)(2,1)S(1)}, bf16[2,4,48,128]{3,2,1,0:T(8,128)(2,1)S(1)}, u32[]{:S(2)}, u32[]{:S(2)}) collective-permute-start(bf16[2,4,48,128]{3,2,1,0:T(8,128)(2,1)S(1)} %pad_maximum_fusion), channel_id=1, source_target_pairs={{0,384},{16,400},{32,416},{48,432},{64,448},{80,464},{96,480},{112... | collective-permute-start | bytes 294920 | tf_op jit(solution)/shard_map/ppermute | solution.py:259
  24.9 2.4 %collective-permute-start.2 = (bf16[2,4,48,128]{3,2,1,0:T(8,128)(2,1)S(1)}, bf16[2,4,48,128]{3,2,1,0:T(8,128)(2,1)S(1)}, u32[]{:S(2)}, u32[]{:S(2)}) collective-permute-start(bf16[2,4,48,128]{3,2,1,0:T(8,128)(2,1)S(1)} %pad_maximum_fusion.1), channel_id=1, source_target_pairs={{0,256},{16,272},{32,288},{48,304},{64,320},{80,336},{96,352},{112... | collective-permute-start | bytes 294920 | tf_op jit(solution)/shard_map/ppermute | solution.py:259
  27.4 0.0 copy-start
  27.4 0.0 copy-start.1
  27.4 2.1 %collective-permute-start.3 = (bf16[2,4,48,128]{3,2,1,0:T(8,128)(2,1)S(1)}, bf16[2,4,48,128]{3,2,1,0:T(8,128)(2,1)S(1)}, u32[]{:S(2)}, u32[]{:S(2)}) collective-permute-start(bf16[2,4,48,128]{3,2,1,0:T(8,128)(2,1)S(1)} %pad_maximum_fusion.2), channel_id=1, source_target_pairs={{0,128},{16,144},{32,160},{48,176},{64,192},{80,208},{96,224},{112... | collective-permute-start | bytes 294920 | tf_op jit(solution)/shard_map/ppermute | solution.py:259
  29.5 3.3 %collective-permute-done.1 = bf16[2,4,48,128]{3,2,1,0:T(8,128)(2,1)S(1)} collective-permute-done((bf16[2,4,48,128]{3,2,1,0:T(8,128)(2,1)S(1)}, bf16[2,4,48,128]{3,2,1,0:T(8,128)(2,1)S(1)}, u32[]{:S(2)}, u32[]{:S(2)}) %collective-permute-start.1) | collective-permute-done | bytes 98336 | tf_op jit(solution)/shard_map/ppermute | solution.py:259
  32.8 0.0 collective-permute-done.2
  32.9 3.2 %collective-permute-done.3 = bf16[2,4,48,128]{3,2,1,0:T(8,128)(2,1)S(1)} collective-permute-done((bf16[2,4,48,128]{3,2,1,0:T(8,128)(2,1)S(1)}, bf16[2,4,48,128]{3,2,1,0:T(8,128)(2,1)S(1)}, u32[]{:S(2)}, u32[]{:S(2)}) %collective-permute-start.3) | collective-permute-done | bytes 98336 | tf_op jit(solution)/shard_map/ppermute | solution.py:259
  36.1 7.9 %collective-permute-start.4 = (bf16[2,4,48,128]{3,2,1,0:T(8,128)(2,1)S(1)}, bf16[2,4,48,128]{3,2,1,0:T(8,128)(2,1)S(1)}, u32[]{:S(2)}, u32[]{:S(2)}) collective-permute-start(bf16[2,4,48,128]{3,2,1,0:T(8,128)(2,1)S(1)} %pad_maximum_fusion.4), channel_id=1, source_target_pairs={{0,64},{16,80},{32,96},{48,112},{64,0},{80,16},{96,32},{112,48},{1... | collective-permute-start | bytes 294920 | tf_op jit(solution)/shard_map/ppermute | solution.py:259
  44.0 2.1 %collective-permute-start.5 = (bf16[2,4,48,128]{3,2,1,0:T(8,128)(2,1)S(1)}, bf16[2,4,48,128]{3,2,1,0:T(8,128)(2,1)S(1)}, u32[]{:S(2)}, u32[]{:S(2)}) collective-permute-start(bf16[2,4,48,128]{3,2,1,0:T(8,128)(2,1)S(1)} %pad_maximum_fusion.5), channel_id=1, source_target_pairs={{0,96},{16,112},{32,64},{48,80},{64,32},{80,48},{96,0},{112,16},{1... | collective-permute-start | bytes 294920 | tf_op jit(solution)/shard_map/ppermute | solution.py:259
  46.1 2.1 %collective-permute-start.6 = (bf16[2,4,48,128]{3,2,1,0:T(8,128)(2,1)S(1)}, bf16[2,4,48,128]{3,2,1,0:T(8,128)(2,1)S(1)}, u32[]{:S(2)}, u32[]{:S(2)}) collective-permute-start(bf16[2,4,48,128]{3,2,1,0:T(8,128)(2,1)S(1)} %fusion.5), channel_id=1, source_target_pairs={{0,32},{16,48},{32,0},{48,16},{64,96},{80,112},{96,64},{112,80},{1... | collective-permute-start | bytes 294920 | tf_op jit(solution)/shard_map/ppermute | solution.py:259
  48.2 0.0 all-to-all-done.y_ref
  48.2 10.2 %all-gather = bf16[128,16,128]{2,1,0:T(8,128)(2,1)S(1)} all-gather(bf16[32,16,128]{2,1,0:T(8,128)(2,1)S(1)} %slice.132), channel_id=2, replica_groups={{0,16,128,144},{32,48,160,176},{64,80,192,208},{96,112,224,240},{256,27..., dimensions={0}, use_global_device_ids=true | all-gather | bytes 655360 | tf_op jit(solution)/shard_map/all_gather | solution.py:296
  58.4 0.0 copy-done
  58.4 0.0 copy-done.1
  58.4 3.7 %conv_probs.1.probs_ref = bf16[16,256,128]{2,1,0:T(8,128)(2,1)S(1)} custom-call(bf16[32,160,128]{2,1,0:T(8,128)(2,1)S(1)} %all-to-all-done.y_ref, bf16[4,32,16,128]{3,2,1,0:T(8,128)(2,1)S(1)} %bitcast.24, bf16[512,512]{1,0:T(8,128)(2,1)S(1)} %copy-done.1, bf16[2,256,512]{2,1,0:T(8,128)(2,1)S(1)} %copy-done), custom_call_target="tpu_custom_call" | custom-call | flops 5368709120 | bytes 5242880 | tf_op jit(solution)/shard_map/conv_probs/pallas_call | solution.py:298
  62.1 0.0 collective-permute-done.4.refs_1_
  62.1 0.0 collective-permute-done.5.refs_2_
  62.1 0.0 collective-permute-done.6.refs_3_
  62.1 0.5 mix.1
  62.6 25.9 %all_to_all.10 = bf16[32,64,128]{2,1,0:T(8,128)(2,1)S(1)} all-to-all(bf16[32,64,128]{2,1,0:T(8,128)(2,1)S(1)} %mix.1), channel_id=1, replica_groups=mesh['context'=32,'dp'=16] {'context'}, dimensions={0} | all-to-all | bytes 1048576 | tf_op jit(solution)/shard_map/all_to_all | solution.py:323
  88.5 0.9 copy_bitcast_fusion
  (14 shorter events, 0.2 us)
Async XLA Ops:
  2.3 14.6 %copy-start.3 = (bf16[16,48,128]{2,1,0:T(8,128)(2,1)S(1)}, bf16[16,48,128]{2,1,0:T(8,128)(2,1)}, u32[]{:S(2)}) copy-start(bf16[16,48,128]{2,1,0:T(8,128)(2,1)} %get-tuple-element.10) | copy-start | bytes 589828
  2.4 16.8 %copy-start.2 = (bf16[16,48,128]{2,1,0:T(8,128)(2,1)S(1)}, bf16[16,48,128]{2,1,0:T(8,128)(2,1)}, u32[]{:S(2)}) copy-start(bf16[16,48,128]{2,1,0:T(8,128)(2,1)} %get-tuple-element.9) | copy-start | bytes 589828
  2.4 45.8 %all-to-all-start = ((bf16[32,160,128]{2,1,0:T(8,128)(2,1)}), bf16[32,160,128]{2,1,0:T(8,128)(2,1)S(1)}, u32[]{:S(2)}, u32[]{:S(2)}) async-start(bf16[32,160,128]{2,1,0:T(8,128)(2,1)} %get-tuple-element.8), calls=%async_computation | async-start | bytes 2621440 | tf_op jit(solution)/shard_map/all_to_all | solution.py:292
  16.9 3.3 %collective-permute-start = (bf16[16,48,128]{2,1,0:T(8,128)(2,1)S(1)}, bf16[16,48,128]{2,1,0:T(8,128)(2,1)S(1)}, u32[]{:S(2)}, u32[]{:S(2)}) collective-permute-start(bf16[16,48,128]{2,1,0:T(8,128)(2,1)S(1)} %copy-done.3), channel_id=1, source_target_pairs={{0,16},{16,0},{32,48},{48,32},{64,80},{80,64},{96,112},{112,96},{1... | collective-permute-start | bytes 589832 | tf_op jit(solution)/shard_map/ppermute | solution.py:259
  20.3 12.5 %collective-permute-start.1 = (bf16[2,4,48,128]{3,2,1,0:T(8,128)(2,1)S(1)}, bf16[2,4,48,128]{3,2,1,0:T(8,128)(2,1)S(1)}, u32[]{:S(2)}, u32[]{:S(2)}) collective-permute-start(bf16[2,4,48,128]{3,2,1,0:T(8,128)(2,1)S(1)} %pad_maximum_fusion), channel_id=1, source_target_pairs={{0,384},{16,400},{32,416},{48,432},{64,448},{80,464},{96,480},{112... | collective-permute-start | bytes 294920 | tf_op jit(solution)/shard_map/ppermute | solution.py:259
  24.9 8.0 %collective-permute-start.2 = (bf16[2,4,48,128]{3,2,1,0:T(8,128)(2,1)S(1)}, bf16[2,4,48,128]{3,2,1,0:T(8,128)(2,1)S(1)}, u32[]{:S(2)}, u32[]{:S(2)}) collective-permute-start(bf16[2,4,48,128]{3,2,1,0:T(8,128)(2,1)S(1)} %pad_maximum_fusion.1), channel_id=1, source_target_pairs={{0,256},{16,272},{32,288},{48,304},{64,320},{80,336},{96,352},{112... | collective-permute-start | bytes 294920 | tf_op jit(solution)/shard_map/ppermute | solution.py:259
  27.4 31.0 %copy-start = (bf16[2,256,512]{2,1,0:T(8,128)(2,1)S(1)}, bf16[2,256,512]{2,1,0:T(8,128)(2,1)}, u32[]{:S(2)}) copy-start(bf16[2,256,512]{2,1,0:T(8,128)(2,1)} %constant.11.clone.inv_ref) | copy-start | bytes 1572868
  27.4 31.0 %copy-start.1 = (bf16[512,512]{1,0:T(8,128)(2,1)S(1)}, bf16[512,512]{1,0:T(8,128)(2,1)}, u32[]{:S(2)}) copy-start(bf16[512,512]{1,0:T(8,128)(2,1)} %constant.10.clone.fwd_ref) | copy-start | bytes 1572868
  27.4 8.7 %collective-permute-start.3 = (bf16[2,4,48,128]{3,2,1,0:T(8,128)(2,1)S(1)}, bf16[2,4,48,128]{3,2,1,0:T(8,128)(2,1)S(1)}, u32[]{:S(2)}, u32[]{:S(2)}) collective-permute-start(bf16[2,4,48,128]{3,2,1,0:T(8,128)(2,1)S(1)} %pad_maximum_fusion.2), channel_id=1, source_target_pairs={{0,128},{16,144},{32,160},{48,176},{64,192},{80,208},{96,224},{112... | collective-permute-start | bytes 294920 | tf_op jit(solution)/shard_map/ppermute | solution.py:259
  36.1 25.9 %collective-permute-start.4 = (bf16[2,4,48,128]{3,2,1,0:T(8,128)(2,1)S(1)}, bf16[2,4,48,128]{3,2,1,0:T(8,128)(2,1)S(1)}, u32[]{:S(2)}, u32[]{:S(2)}) collective-permute-start(bf16[2,4,48,128]{3,2,1,0:T(8,128)(2,1)S(1)} %pad_maximum_fusion.4), channel_id=1, source_target_pairs={{0,64},{16,80},{32,96},{48,112},{64,0},{80,16},{96,32},{112,48},{1... | collective-permute-start | bytes 294920 | tf_op jit(solution)/shard_map/ppermute | solution.py:259
  44.0 18.1 %collective-permute-start.5 = (bf16[2,4,48,128]{3,2,1,0:T(8,128)(2,1)S(1)}, bf16[2,4,48,128]{3,2,1,0:T(8,128)(2,1)S(1)}, u32[]{:S(2)}, u32[]{:S(2)}) collective-permute-start(bf16[2,4,48,128]{3,2,1,0:T(8,128)(2,1)S(1)} %pad_maximum_fusion.5), channel_id=1, source_target_pairs={{0,96},{16,112},{32,64},{48,80},{64,32},{80,48},{96,0},{112,16},{1... | collective-permute-start | bytes 294920 | tf_op jit(solution)/shard_map/ppermute | solution.py:259
  46.1 16.0 %collective-permute-start.6 = (bf16[2,4,48,128]{3,2,1,0:T(8,128)(2,1)S(1)}, bf16[2,4,48,128]{3,2,1,0:T(8,128)(2,1)S(1)}, u32[]{:S(2)}, u32[]{:S(2)}) collective-permute-start(bf16[2,4,48,128]{3,2,1,0:T(8,128)(2,1)S(1)} %fusion.5), channel_id=1, source_target_pairs={{0,32},{16,48},{32,0},{48,16},{64,96},{80,112},{96,64},{112,80},{1... | collective-permute-start | bytes 294920 | tf_op jit(solution)/shard_map/ppermute | solution.py:259
